TPU v7x, 32 devices: a whole 2x2x4 slice. The times are simulated.
32 devices in a mesh: groups: 2 (over x), seq: 16 (over z, y, core).
Axes of the slice: x: 2, y: 2, z: 4, core: 2. Of those that a mesh axis runs over, the one named last changes fastest.
Arguments:
- tile_heads: bfloat16 [8192, 1536], P(('groups', 'seq')), parts along dimension 0, may hold values from -6 to 6
- tile_stream: bfloat16 [8192, 1536], P(('groups', 'seq')), parts along dimension 0, may hold values from -6 to 6
- tissue_counts: int32 [32], P('groups'), parts along dimension 0, may hold values from 1 to 256, 2048 in all
- head_weight: bfloat16 [1536, 1536], replicated, may hold values from -0.15625 to 0.15625
- stream_scale: float32 [1536], replicated, may hold values from 0.3 to 3
- final_gain: float32 [1536], replicated, may hold values from 0.1 to 1.9
- final_bias: float32 [1536], replicated, may hold values from -3 to 3
- embed_weight: bfloat16 [1536, 768], replicated, may hold values from -0.15625 to 0.15625
- embed_bias: float32 [768], replicated, may hold values from -3 to 3
- slide_gain: float32 [768], replicated, may hold values from 0.1 to 1.9
- triple_weight: bfloat16 [768, 1152], replicated, may hold values from -4 to 4
- inner_gain: float32 [384], replicated, may hold values from 0.1 to 1.9
- output_weight: bfloat16 [384, 768], replicated, may hold values from -0.3125 to 0.3125
Outputs:
- attended: bfloat16 [4096, 768], P(('groups', 'seq')), parts along dimension 0
There are 2 independent parts, one for each index of `groups`. A program takes and returns all parts, laid end to end along the dimension named above; an argument that names none is the same for every part. Nothing has to cross between parts.
Inputs may be any that keep to these rules, and one draw needn't show every extreme that they name: `tissue_counts`: the counts sum to 2048; some loader holds exactly 256 tiles.
All inputs are finite; a program needn't handle non-finite values.
Results may differ from a plain program's by a relative error of at most 0.017.
Values may be sent and summed in bfloat16 or wider, within the bound.
A program may use at most 128 MiB of HBM per device.

v0:
```python
import math

import jax
import jax.numpy as jnp
import numpy as np
from jax import lax
from jax.sharding import PartitionSpec as P

HEAD_DIM = 48
HEADS = 8
BRANCHES = 5
SEG_BASE = 1024
TILE_DEV = 128


EPSILON = 1e-06
NEGATIVE = -1e30


def swapped(block, axis, stride):
    count = lax.axis_size(axis)
    route = []
    for low in range(count):
        high = low | 1 << stride
        if high != low and high < count:
            route += [(low, high), (high, low)]
    return lax.ppermute(block, axis, route)


def layer_norm(values, gain_vector):
    average = jnp.mean(values, axis=-1, keepdims=True)
    centred = values - average
    spread = jnp.mean(centred * centred, axis=-1, keepdims=True)
    return centred * lax.rsqrt(spread + EPSILON) * gain_vector


def encode(head_rows, stream_rows, head_weight, stream_scale, final_gain, final_bias):
    blended = jnp.dot(head_rows, head_weight, preferred_element_type=jnp.float32)
    summed = stream_rows.astype(jnp.float32) + stream_scale * blended
    return (layer_norm(summed, final_gain) + final_bias).astype(jnp.bfloat16)


def project(embedding, embed_weight, embed_bias):
    return (
        jnp.dot(embedding, embed_weight, preferred_element_type=jnp.float32) + embed_bias
    ).astype(jnp.bfloat16)


def member_table(stride):
    return np.arange(stride)[:, None] == (np.arange(HEADS) % stride)[None, :]


def select_heads(source, stride):
    shaped = source.reshape(source.shape[0] // stride, stride, HEADS, source.shape[-1])
    member = member_table(stride)[None, :, :, None]
    return jnp.sum(jnp.where(member, shaped, jnp.zeros((), shaped.dtype)), axis=1)


def spread_heads(values, stride, fill_value):
    member = member_table(stride)
    if values.ndim == 3:
        member = member[:, :, None]
    member = member[None]
    placed = jnp.where(member, values[:, None], jnp.asarray(fill_value, values.dtype))
    return placed.reshape((values.shape[0] * stride,) + values.shape[1:])


def local(
    tile_heads,
    tile_stream,
    tissue_counts,
    head_weight,
    stream_scale,
    final_gain,
    final_bias,
    embed_weight,
    embed_bias,
    slide_gain,
    triple_weight,
    inner_gain,
    output_weight,
):
    devices = lax.axis_size("seq")
    rank_here = lax.axis_index("seq")
    capacity = tile_heads.shape[0] // devices
    per_peer = TILE_DEV // devices
    starts = jnp.cumsum(tissue_counts) - tissue_counts
    own_start = starts[rank_here]

    def outbound(source):
        shaped = source.reshape(capacity, devices, source.shape[-1])
        return jnp.roll(shaped, own_start % devices, axis=1)

    column = jnp.remainder(rank_here - starts, devices)
    slot_ids = jnp.arange(capacity, dtype=jnp.int32)[:, None] * devices + column[None, :]
    filled = slot_ids < tissue_counts[None, :]
    home_slot = (starts[None, :] + slot_ids) // devices
    target = jnp.where(filled, home_slot, TILE_DEV).reshape(capacity * devices)

    def place_rows(arrived):
        flattened = arrived.reshape(capacity * devices, arrived.shape[-1])
        return (
            jnp.zeros((TILE_DEV, flattened.shape[-1]), flattened.dtype)
            .at[target]
            .set(flattened, mode="drop")
        )

    head_in, stream_in = (
        lax.all_to_all(outbound(tile_heads), "seq", split_axis=1, concat_axis=1, tiled=True),
        lax.all_to_all(outbound(tile_stream), "seq", split_axis=1, concat_axis=1, tiled=True),
    )
    embedding = encode(
        place_rows(head_in),
        place_rows(stream_in),
        head_weight,
        stream_scale,
        final_gain,
        final_bias,
    )
    back_home = lax.all_to_all(
        embedding.reshape(devices, per_peer, 1, embedding.shape[-1]),
        "seq",
        split_axis=0,
        concat_axis=2,
        tiled=True,
    )
    slide_rows = project(back_home.reshape(TILE_DEV, embedding.shape[-1]), embed_weight, embed_bias)
    normed = layer_norm(slide_rows.astype(jnp.float32), slide_gain).astype(jnp.bfloat16)
    triple = jnp.dot(normed, triple_weight, preferred_element_type=jnp.float32).astype(jnp.bfloat16)
    inner_width = HEADS * HEAD_DIM
    queries = triple[:, :inner_width].reshape(TILE_DEV, HEADS, HEAD_DIM)
    key_value = jnp.concatenate(
        [
            triple[:, inner_width : 2 * inner_width].reshape(TILE_DEV, HEADS, HEAD_DIM),
            triple[:, 2 * inner_width :].reshape(TILE_DEV, HEADS, HEAD_DIM),
        ],
        axis=2,
    )
    total_rows = TILE_DEV * devices
    strides = [2**branch for branch in range(BRANCHES)]
    depths = [
        (min(SEG_BASE * stride, total_rows) // TILE_DEV).bit_length() - 1 for stride in strides
    ]
    blocks = [
        select_heads(key_value, stride).reshape(TILE_DEV // stride, 2 * inner_width)
        for stride in strides
    ]
    gathered = []
    for branch in range(BRANCHES):
        current = blocks[branch]
        for bit_place in range(depths[branch]):
            partner = swapped(current, "seq", bit_place)
            current = jnp.concatenate([current, partner], axis=0)
        gathered.append(current)
    scaling = 1.0 / math.sqrt(HEAD_DIM)
    high_list, total_list, mix_list = ([], [], [])
    for branch in range(BRANCHES):
        stride = strides[branch]
        own_queries = select_heads(queries, stride)
        gathered_rows = gathered[branch].reshape(-1, HEADS, 2 * HEAD_DIM)
        scores = (
            jnp.einsum(
                "qhd,khd->hqk",
                own_queries,
                gathered_rows[:, :, :HEAD_DIM],
                preferred_element_type=jnp.float32,
            )
            * scaling
        )
        highest = jnp.max(scores, axis=2)
        weights = jnp.exp(scores - highest[:, :, None])
        summed = jnp.sum(weights, axis=2)
        blended = jnp.einsum(
            "hqk,khd->qhd",
            weights.astype(jnp.bfloat16),
            gathered_rows[:, :, HEAD_DIM:],
            preferred_element_type=jnp.float32,
        )
        high_list.append(spread_heads(highest.T, stride, NEGATIVE))
        total_list.append(spread_heads(summed.T, stride, 0.0))
        mix_list.append(spread_heads(blended, stride, 0.0))
    high_all = jnp.stack(high_list)
    summit = jnp.max(high_all, axis=0)
    factor = jnp.exp(high_all - summit)
    denominator = jnp.sum(jnp.stack(total_list) * factor, axis=0)
    numerator = jnp.sum(jnp.stack(mix_list) * factor[..., None], axis=0)
    mixed = (numerator / denominator[..., None]).reshape(TILE_DEV, inner_width)
    inner = layer_norm(mixed, inner_gain).astype(jnp.bfloat16)
    return jnp.dot(inner, output_weight, preferred_element_type=jnp.float32).astype(jnp.bfloat16)


def solution(mesh):
    placed = (
        P(("groups", "seq"), None),
        P(("groups", "seq"), None),
        P("groups"),
        P(),
        P(),
        P(),
        P(),
        P(),
        P(),
        P(),
        P(),
        P(),
        P(),
    )
    return jax.shard_map(
        local, mesh=mesh, in_specs=placed, out_specs=P(("groups", "seq"), None), check_vma=False
    )
```

profile of v0, /device:TPU:0, one launch (start us, length us, event | category | flops | bytes accessed | tf_op | source)
XLA Modules:
  0.0 234.2 jit_solution(11542224513240637843)
XLA Ops:
  4.3 1.7 fusion.20
  6.0 1.3 copy.136
  7.3 7.5 %all-to-all-start.1 = ((bf16[16,16,1536]{2,0,1:T(8,128)(2,1)}), bf16[16,16,1536]{2,0,1:T(8,128)(2,1)S(1)}, u32[]{:S(2)}, u32[]{:S(2)}) async-start(bf16[16,16,1536]{2,0,1:T(8,128)(2,1)} %copy.136), calls=%async_computation.1 | async-start | bytes 1572864 | tf_op jit(solution)/shard_map/all_to_all | solution.py:109
  14.8 1.7 fusion.21
  16.5 1.3 copy.134
  17.8 15.7 %all-to-all-done.1 = bf16[16,16,1536]{2,0,1:T(8,128)(2,1)S(1)} async-done(((bf16[16,16,1536]{2,0,1:T(8,128)(2,1)}), bf16[16,16,1536]{2,0,1:T(8,128)(2,1)S(1)}, u32[]{:S(2)}, u32[]{:S(2)}) %all-to-all-start.1) | async-done | bytes 786464 | tf_op jit(solution)/shard_map/all_to_all | solution.py:109
  33.5 5.5 %all-to-all-start = ((bf16[16,16,1536]{2,0,1:T(8,128)(2,1)}), bf16[16,16,1536]{2,0,1:T(8,128)(2,1)}, u32[]{:S(2)}, u32[]{:S(2)}) async-start(bf16[16,16,1536]{2,0,1:T(8,128)(2,1)} %copy.134), calls=%async_computation | async-start | bytes 1572864 | tf_op jit(solution)/shard_map/all_to_all | solution.py:110
  39.4 1.3 copy.137
  40.7 2.4 %scatter_custom_fusion.1 = bf16[128,1536]{1,0:T(8,128)(2,1)S(1)} fusion(s32[256]{0:T(256)S(1)} %bitcast.172, bf16[256,1536]{1,0:T(8,128)(2,1)} %bitcast.149, bf16[]{:T(256)} %constant.106.clone.1), kind=kCustom, calls=%fused_computation.92 | custom fusion | bytes 393728 | tf_op jit(solution)/shard_map/scatter | solution.py:105
  43.2 14.6 %all-to-all-done = bf16[16,16,1536]{2,0,1:T(8,128)(2,1)} async-done(((bf16[16,16,1536]{2,0,1:T(8,128)(2,1)}), bf16[16,16,1536]{2,0,1:T(8,128)(2,1)}, u32[]{:S(2)}, u32[]{:S(2)}) %all-to-all-start) | async-done | bytes 786464 | tf_op jit(solution)/shard_map/all_to_all | solution.py:110
  57.8 2.5 %copy.135 = bf16[16,16,1536]{2,1,0:T(8,128)(2,1)} copy(bf16[16,16,1536]{2,0,1:T(8,128)(2,1)} %all-to-all-done) | data formatting | bytes 1572864 | tf_op jit(solution)/shard_map/all_to_all | solution.py:110
  60.3 2.4 %scatter_custom_fusion = bf16[128,1536]{1,0:T(8,128)(2,1)S(1)} fusion(s32[256]{0:T(256)S(1)} %bitcast.173, bf16[256,1536]{1,0:T(8,128)(2,1)} %bitcast.148, bf16[]{:T(256)} %constant.106.clone.1), kind=kCustom, calls=%fused_computation.94 | custom fusion | bytes 393728 | tf_op jit(solution)/shard_map/scatter | solution.py:105
  62.8 3.2 %fusion.73 = (f32[128]{0:T(128)S(1)}, f32[128,1536]{1,0:T(8,128)S(1)}) fusion(bf16[128,1536]{1,0:T(8,128)(2,1)S(1)} %scatter_custom_fusion.1, bf16[1536,1536]{1,0:T(8,128)(2,1)} %param.43, f32[1536]{0:T(1024)S(1)} %copy-done.14, bf16[128,1536]{1,0:T(8,128)(2,1)S(1)} %scatter_custom_fusion), kind=kOutput, calls=%fused_computation.162 | convolution fusion | flops 604766080 | bytes 6298112 | tf_op jit(solution)/shard_map/dot_general | solution.py:38
  67.2 5.5 %all-to-all-start.2 = ((bf16[16,8,1,1536]{3,1,2,0:T(8,128)(2,1)}), bf16[16,8,1,1536]{3,1,2,0:T(8,128)(2,1)S(1)}, u32[]{:S(2)}, u32[]{:S(2)}) async-start(bf16[16,8,1,1536]{3,1,2,0:T(8,128)(2,1)} %fusion.30), calls=%async_computation.2 | async-start | bytes 786432 | tf_op jit(solution)/shard_map/all_to_all | solution.py:120
  75.5 9.5 %all-to-all-done.2 = bf16[16,8,1,1536]{3,1,2,0:T(8,128)(2,1)S(1)} async-done(((bf16[16,8,1,1536]{3,1,2,0:T(8,128)(2,1)}), bf16[16,8,1,1536]{3,1,2,0:T(8,128)(2,1)S(1)}, u32[]{:S(2)}, u32[]{:S(2)}) %all-to-all-start.2) | async-done | bytes 393248 | tf_op jit(solution)/shard_map/all_to_all | solution.py:120
  94.3 1.2 fusion.37
  97.4 1.1 fusion.36
  102.2 1.7 select_reduce_fusion
  103.8 1.7 select_reduce_fusion.1
  106.3 1.8 select_reduce_fusion.3
  108.6 1.1 fusion.34
  109.7 1.1 fusion.35
  114.0 1.2 collective-permute-start.12
  116.7 1.2 collective-permute-start.17
  125.8 2.0 collective-permute-start.4
  127.8 1.8 pad_maximum_fusion.9
  130.0 1.6 pad_maximum_fusion.10
  131.6 2.0 collective-permute-start.14
  133.6 1.7 copy.164
  135.3 1.7 copy.175
  137.0 2.1 concatenate.213
  139.1 1.1 fusion.77
  140.2 1.1 convolution_bitcast_fusion.3
  143.3 1.9 copy.179
  145.2 1.7 pad_maximum_fusion.3
  147.7 1.9 pad_maximum_fusion.4
  150.5 2.1 pad_maximum_fusion.5
  153.4 1.7 copy.165
  155.2 2.1 concatenate.202
  157.3 1.1 fusion.76
  160.8 1.1 convolution_bitcast_fusion.2
  163.7 1.9 copy.170
  165.6 2.0 pad_maximum_fusion.1
  167.6 1.7 collective-permute-start.2
  169.4 2.1 pad_maximum_fusion.2
  171.5 1.5 collective-permute-start.6
  172.9 2.1 concatenate.191
  175.1 1.3 fusion.75
  176.4 1.3 convolution_bitcast_fusion.1
  183.3 17.7 %collective-permute-done.2 = bf16[512,768]{0,1:T(8,128)(2,1)} collective-permute-done((bf16[512,768]{0,1:T(8,128)(2,1)}, bf16[512,768]{0,1:T(8,128)(2,1)}, u32[]{:S(2)}, u32[]{:S(2)}) %collective-permute-start.2) | collective-permute-done | bytes 786464 | tf_op jit(solution)/shard_map/ppermute | solution.py:27
  200.9 1.5 pad_maximum_fusion
  205.4 1.6 fusion.14
  207.0 3.8 %concatenate.180 = bf16[1024,8,96]{0,2,1:T(8,128)(2,1)} concatenate(bf16[64,8,96]{0,2,1:T(8,128)(2,1)S(1)} %copy.148, bf16[64,8,96]{0,2,1:T(8,128)(2,1)S(1)} %bitcast.131, bf16[128,8,96]{0,2,1:T(8,128)(2,1)} %bitcast.22, bf16[256,8,96]{0,2,1:T(8,128)(2,1)} %bitcast.23, bf16[512,8,96]{0,2,1:T(8,128)(2,1)} %bitcast.24), dimensions={0} | concatenate | bytes 3145728 | tf_op jit(solution)/shard_map/concatenate | solution.py:153
  210.8 1.7 multiply_reduce_fusion.1
  216.3 1.3 constant_dynamic-update-slice_fusion.3
  217.6 1.3 constant_dynamic-update-slice_fusion.2
  218.9 1.3 constant_dynamic-update-slice_fusion.1
  220.8 1.3 constant_dynamic-update-slice_fusion.8
  222.0 1.3 constant_dynamic-update-slice_fusion.7
  224.5 1.3 select_dynamic-update-slice_fusion.3
  225.8 1.6 select_dynamic-update-slice_fusion.2
  227.4 1.4 select_dynamic-update-slice_fusion.1
  228.8 1.3 select_dynamic-update-slice_fusion
  231.6 1.3 multiply_reduce_fusion.2
  (206 shorter events, 60.9 us)
Async XLA Ops:
  0.0 85.0 %copy-start = (bf16[1536,768]{1,0:T(8,128)(2,1)S(1)}, bf16[1536,768]{1,0:T(8,128)(2,1)}, u32[]{:S(2)}) copy-start(bf16[1536,768]{1,0:T(8,128)(2,1)} %param.47) | copy-start | bytes 7077892
  7.3 26.2 %all-to-all-start.1 = ((bf16[16,16,1536]{2,0,1:T(8,128)(2,1)}), bf16[16,16,1536]{2,0,1:T(8,128)(2,1)S(1)}, u32[]{:S(2)}, u32[]{:S(2)}) async-start(bf16[16,16,1536]{2,0,1:T(8,128)(2,1)} %copy.136), calls=%async_computation.1 | async-start | bytes 1572864 | tf_op jit(solution)/shard_map/all_to_all | solution.py:109
  14.8 24.3 %copy-start.21 = (s32[16]{0:T(128)S(1)}, s32[16]{0:T(128)}, u32[]{:S(2)}) copy-start(s32[16]{0:T(128)} %param.42) | copy-start | bytes 196
  33.5 24.3 %all-to-all-start = ((bf16[16,16,1536]{2,0,1:T(8,128)(2,1)}), bf16[16,16,1536]{2,0,1:T(8,128)(2,1)}, u32[]{:S(2)}, u32[]{:S(2)}) async-start(bf16[16,16,1536]{2,0,1:T(8,128)(2,1)} %copy.134), calls=%async_computation | async-start | bytes 1572864 | tf_op jit(solution)/shard_map/all_to_all | solution.py:110
  39.0 23.7 %copy-start.14 = (f32[1536]{0:T(1024)S(1)}, f32[1536]{0:T(1024)}, u32[]{:S(2)}) copy-start(f32[1536]{0:T(1024)} %param.44) | copy-start | bytes 18436
  62.7 3.5 %copy-start.15 = (f32[1536]{0:T(1024)S(1)}, f32[1536]{0:T(1024)}, u32[]{:S(2)}) copy-start(f32[1536]{0:T(1024)} %param.46) | copy-start | bytes 18436
  62.7 3.5 %copy-start.16 = (f32[1536]{0:T(1024)S(1)}, f32[1536]{0:T(1024)}, u32[]{:S(2)}) copy-start(f32[1536]{0:T(1024)} %param.45) | copy-start | bytes 18436
  66.0 6.8 %copy-start.27 = (pred[16,8]{0,1:T(8,128)(4,1)S(1)}, pred[16,8]{0,1:T(8,128)(4,1)}, u32[]{:S(2)}) copy-start(pred[16,8]{0,1:T(8,128)(4,1)} %constant.141) | copy-start | bytes 388
  66.0 7.4 %copy-start.25 = (pred[8,8]{0,1:T(8,128)(4,1)S(1)}, pred[8,8]{0,1:T(8,128)(4,1)}, u32[]{:S(2)}) copy-start(pred[8,8]{0,1:T(8,128)(4,1)} %constant.134) | copy-start | bytes 196
  66.0 8.1 %copy-start.20 = (pred[4,8]{1,0:T(4,128)(4,1)S(1)}, pred[4,8]{1,0:T(4,128)(4,1)}, u32[]{:S(2)}) copy-start(pred[4,8]{1,0:T(4,128)(4,1)} %constant.133) | copy-start | bytes 100
  66.0 8.8 %copy-start.18 = (pred[2,8]{1,0:T(4,128)(4,1)S(1)}, pred[2,8]{1,0:T(4,128)(4,1)}, u32[]{:S(2)}) copy-start(pred[2,8]{1,0:T(4,128)(4,1)} %constant.132) | copy-start | bytes 52
  66.0 19.0 %copy-start.22 = (f32[768]{0:T(1024)S(1)}, f32[768]{0:T(1024)}, u32[]{:S(2)}) copy-start(f32[768]{0:T(1024)} %param.48) | copy-start | bytes 9220
  67.2 17.7 %all-to-all-start.2 = ((bf16[16,8,1,1536]{3,1,2,0:T(8,128)(2,1)}), bf16[16,8,1,1536]{3,1,2,0:T(8,128)(2,1)S(1)}, u32[]{:S(2)}, u32[]{:S(2)}) async-start(bf16[16,8,1,1536]{3,1,2,0:T(8,128)(2,1)} %fusion.30), calls=%async_computation.2 | async-start | bytes 786432 | tf_op jit(solution)/shard_map/all_to_all | solution.py:120
  75.5 10.4 %copy-start.23 = (f32[768]{0:T(1024)S(1)}, f32[768]{0:T(1024)}, u32[]{:S(2)}) copy-start(f32[768]{0:T(1024)} %param.49) | copy-start | bytes 9220
  84.9 1.5 copy-start.2
  86.9 7.4 %copy-start.17 = (pred[16,8]{1,0:T(8,128)(4,1)S(1)}, pred[16,8]{1,0:T(8,128)(4,1)}, u32[]{:S(2)}) copy-start(pred[16,8]{1,0:T(8,128)(4,1)} %constant.135) | copy-start | bytes 388
  87.1 14.3 %copy-start.4 = (bf16[128,384]{0,1:T(8,128)(2,1)}, bf16[128,384]{0,1:T(8,128)(2,1)S(1)}, u32[]{:S(2)}) copy-start(bf16[128,384]{0,1:T(8,128)(2,1)S(1)} %copy.140) | copy-start | bytes 294916
  88.3 9.1 %copy-start.24 = (pred[8,8]{1,0:T(8,128)(4,1)S(1)}, pred[8,8]{1,0:T(8,128)(4,1)}, u32[]{:S(2)}) copy-start(pred[8,8]{1,0:T(8,128)(4,1)} %constant.140) | copy-start | bytes 196
  93.4 12.9 %copy-start.5 = (bf16[128,384]{0,1:T(8,128)(2,1)}, bf16[128,384]{0,1:T(8,128)(2,1)S(1)}, u32[]{:S(2)}) copy-start(bf16[128,384]{0,1:T(8,128)(2,1)S(1)} %copy.141) | copy-start | bytes 294916
  101.3 8.4 %copy-start.3 = (bf16[32,4,8,48]{3,2,1,0:T(8,128)(2,1)S(1)}, bf16[32,4,8,48]{3,2,1,0:T(8,128)(2,1)}, u32[]{:S(2)}) copy-start(bf16[32,4,8,48]{3,2,1,0:T(8,128)(2,1)} %concatenate.182) | copy-start | bytes 294916
  102.0 43.1 %collective-permute-start = (bf16[128,768]{0,1:T(8,128)(2,1)}, bf16[128,768]{0,1:T(8,128)(2,1)S(1)}, u32[]{:S(2)}, u32[]{:S(2)}) collective-permute-start(bf16[128,768]{0,1:T(8,128)(2,1)} %bitcast.14), channel_id=1, source_target_pairs={{0,1},{1,0},{2,3},{3,2},{4,5},{5,4},{6,7},{7,6},{8,9},{9,8},{10,11... | collective-permute-start | bytes 589832 | tf_op jit(solution)/shard_map/ppermute | solution.py:27
  108.1 3.7 %collective-permute-start.15 = (bf16[8,768]{1,0:T(8,128)(2,1)S(1)}, bf16[8,768]{1,0:T(8,128)(2,1)S(1)}, u32[]{:S(2)}, u32[]{:S(2)}) collective-permute-start(bf16[8,768]{1,0:T(8,128)(2,1)S(1)} %reshape.654), channel_id=1, source_target_pairs={{0,1},{1,0},{2,3},{3,2},{4,5},{5,4},{6,7},{7,6},{8,9},{9,8},{10,11... | collective-permute-start | bytes 36872 | tf_op jit(solution)/shard_map/ppermute | solution.py:27
  108.5 5.0 %collective-permute-start.11 = (bf16[16,768]{1,0:T(8,128)(2,1)S(1)}, bf16[16,768]{1,0:T(8,128)(2,1)S(1)}, u32[]{:S(2)}, u32[]{:S(2)}) collective-permute-start(bf16[16,768]{1,0:T(8,128)(2,1)S(1)} %reshape.653), channel_id=1, source_target_pairs={{0,1},{1,0},{2,3},{3,2},{4,5},{5,4},{6,7},{7,6},{8,9},{9,8},{10,11... | collective-permute-start | bytes 73736 | tf_op jit(solution)/shard_map/ppermute | solution.py:27
  111.2 13.8 %collective-permute-start.3 = (bf16[64,768]{0,1:T(8,128)(2,1)S(1)}, bf16[64,768]{0,1:T(8,128)(2,1)S(1)}, u32[]{:S(2)}, u32[]{:S(2)}) collective-permute-start(bf16[64,768]{0,1:T(8,128)(2,1)S(1)} %bitcast.123), channel_id=1, source_target_pairs={{0,1},{1,0},{2,3},{3,2},{4,5},{5,4},{6,7},{7,6},{8,9},{9,8},{10,11... | collective-permute-start | bytes 294920 | tf_op jit(solution)/shard_map/ppermute | solution.py:27
  111.7 7.0 %collective-permute-start.7 = (bf16[32,768]{0,1:T(8,128)(2,1)S(1)}, bf16[32,768]{0,1:T(8,128)(2,1)S(1)}, u32[]{:S(2)}, u32[]{:S(2)}) collective-permute-start(bf16[32,768]{0,1:T(8,128)(2,1)S(1)} %bitcast.127), channel_id=1, source_target_pairs={{0,1},{1,0},{2,3},{3,2},{4,5},{5,4},{6,7},{7,6},{8,9},{9,8},{10,11... | collective-permute-start | bytes 147464 | tf_op jit(solution)/shard_map/ppermute | solution.py:27
  111.8 4.3 %collective-permute-start.16 = (bf16[16,768]{1,0:T(8,128)(2,1)S(1)}, bf16[16,768]{1,0:T(8,128)(2,1)S(1)}, u32[]{:S(2)}, u32[]{:S(2)}) collective-permute-start(bf16[16,768]{1,0:T(8,128)(2,1)S(1)} %pad_maximum_fusion.15), channel_id=1, source_target_pairs={{0,2},{2,0},{1,3},{3,1},{4,6},{6,4},{5,7},{7,5},{8,10},{10,8},{9,1... | collective-permute-start | bytes 73736 | tf_op jit(solution)/shard_map/ppermute | solution.py:27
  114.0 6.2 %collective-permute-start.12 = (bf16[32,768]{1,0:T(8,128)(2,1)}, bf16[32,768]{1,0:T(8,128)(2,1)S(1)}, u32[]{:S(2)}, u32[]{:S(2)}) collective-permute-start(bf16[32,768]{1,0:T(8,128)(2,1)} %pad_maximum_fusion.13), channel_id=1, source_target_pairs={{0,2},{2,0},{1,3},{3,1},{4,6},{6,4},{5,7},{7,5},{8,10},{10,8},{9,1... | collective-permute-start | bytes 147464 | tf_op jit(solution)/shard_map/ppermute | solution.py:27
  116.7 5.9 %collective-permute-start.17 = (bf16[32,768]{1,0:T(8,128)(2,1)}, bf16[32,768]{1,0:T(8,128)(2,1)S(1)}, u32[]{:S(2)}, u32[]{:S(2)}) collective-permute-start(bf16[32,768]{1,0:T(8,128)(2,1)} %pad_maximum_fusion.14), channel_id=1, source_target_pairs={{0,4},{4,0},{1,5},{5,1},{2,6},{6,2},{3,7},{7,3},{8,12},{12,8},{9,1... | collective-permute-start | bytes 147464 | tf_op jit(solution)/shard_map/ppermute | solution.py:27
  119.4 8.3 %collective-permute-start.8 = (bf16[64,768]{0,1:T(8,128)(2,1)}, bf16[64,768]{0,1:T(8,128)(2,1)}, u32[]{:S(2)}, u32[]{:S(2)}) collective-permute-start(bf16[64,768]{0,1:T(8,128)(2,1)} %pad_maximum_fusion.8), channel_id=1, source_target_pairs={{0,2},{2,0},{1,3},{3,1},{4,6},{6,4},{5,7},{7,5},{8,10},{10,8},{9,1... | collective-permute-start | bytes 294920 | tf_op jit(solution)/shard_map/ppermute | solution.py:27
  120.9 9.1 %collective-permute-start.13 = (bf16[64,768]{1,0:T(8,128)(2,1)}, bf16[64,768]{1,0:T(8,128)(2,1)}, u32[]{:S(2)}, u32[]{:S(2)}) collective-permute-start(bf16[64,768]{1,0:T(8,128)(2,1)} %pad_maximum_fusion.11), channel_id=1, source_target_pairs={{0,4},{4,0},{1,5},{5,1},{2,6},{6,2},{3,7},{7,3},{8,12},{12,8},{9,1... | collective-permute-start | bytes 294920 | tf_op jit(solution)/shard_map/ppermute | solution.py:27
  123.3 18.3 %copy-start.28 = (pred[16,8]{0,1:T(8,128)(4,1)S(1)}, pred[16,8]{0,1:T(8,128)(4,1)}, u32[]{:S(2)}) copy-start(pred[16,8]{0,1:T(8,128)(4,1)} %constant.141) | copy-start | bytes 388
  123.3 12.0 %collective-permute-start.18 = (bf16[64,768]{1,0:T(8,128)(2,1)}, bf16[64,768]{1,0:T(8,128)(2,1)}, u32[]{:S(2)}, u32[]{:S(2)}) collective-permute-start(bf16[64,768]{1,0:T(8,128)(2,1)} %pad_maximum_fusion.12), channel_id=1, source_target_pairs={{0,8},{8,0},{1,9},{9,1},{2,10},{10,2},{3,11},{11,3},{4,12},{12,4},... | collective-permute-start | bytes 294920 | tf_op jit(solution)/shard_map/ppermute | solution.py:27
  125.8 22.0 %collective-permute-start.4 = (bf16[128,768]{0,1:T(8,128)(2,1)}, bf16[128,768]{0,1:T(8,128)(2,1)}, u32[]{:S(2)}, u32[]{:S(2)}) collective-permute-start(bf16[128,768]{0,1:T(8,128)(2,1)} %pad_maximum_fusion.7), channel_id=1, source_target_pairs={{0,2},{2,0},{1,3},{3,1},{4,6},{6,4},{5,7},{7,5},{8,10},{10,8},{9,1... | collective-permute-start | bytes 589832 | tf_op jit(solution)/shard_map/ppermute | solution.py:27
  129.6 20.9 %collective-permute-start.9 = (bf16[128,768]{0,1:T(8,128)(2,1)}, bf16[128,768]{0,1:T(8,128)(2,1)}, u32[]{:S(2)}, u32[]{:S(2)}) collective-permute-start(bf16[128,768]{0,1:T(8,128)(2,1)} %pad_maximum_fusion.9), channel_id=1, source_target_pairs={{0,4},{4,0},{1,5},{5,1},{2,6},{6,2},{3,7},{7,3},{8,12},{12,8},{9,1... | collective-permute-start | bytes 589832 | tf_op jit(solution)/shard_map/ppermute | solution.py:27
  131.6 21.8 %collective-permute-start.14 = (bf16[128,768]{1,0:T(8,128)(2,1)}, bf16[128,768]{1,0:T(8,128)(2,1)}, u32[]{:S(2)}, u32[]{:S(2)}) collective-permute-start(bf16[128,768]{1,0:T(8,128)(2,1)} %pad_maximum_fusion.10), channel_id=1, source_target_pairs={{0,8},{8,0},{1,9},{9,1},{2,10},{10,2},{3,11},{11,3},{4,12},{12,4},... | collective-permute-start | bytes 589832 | tf_op jit(solution)/shard_map/ppermute | solution.py:27
  146.9 10.4 %copy-start.12 = (bf16[16,8,48]{2,1,0:T(8,128)(2,1)S(1)}, bf16[16,8,48]{2,1,0:T(8,128)(2,1)}, u32[]{:S(2)}) copy-start(bf16[16,8,48]{2,1,0:T(8,128)(2,1)} %select_reduce_fusion.1) | copy-start | bytes 36868
  146.9 11.8 %copy-start.26 = (pred[8,8]{0,1:T(8,128)(4,1)S(1)}, pred[8,8]{0,1:T(8,128)(4,1)}, u32[]{:S(2)}) copy-start(pred[8,8]{0,1:T(8,128)(4,1)} %constant.134) | copy-start | bytes 196
  146.9 18.7 %collective-permute-start.1 = (bf16[256,768]{0,1:T(8,128)(2,1)}, bf16[256,768]{0,1:T(8,128)(2,1)}, u32[]{:S(2)}, u32[]{:S(2)}) collective-permute-start(bf16[256,768]{0,1:T(8,128)(2,1)} %pad_maximum_fusion.3), channel_id=1, source_target_pairs={{0,2},{2,0},{1,3},{3,1},{4,6},{6,4},{5,7},{7,5},{8,10},{10,8},{9,1... | collective-permute-start | bytes 1179656 | tf_op jit(solution)/shard_map/ppermute | solution.py:27
  149.6 19.8 %collective-permute-start.5 = (bf16[256,768]{0,1:T(8,128)(2,1)}, bf16[256,768]{0,1:T(8,128)(2,1)}, u32[]{:S(2)}, u32[]{:S(2)}) collective-permute-start(bf16[256,768]{0,1:T(8,128)(2,1)} %pad_maximum_fusion.4), channel_id=1, source_target_pairs={{0,4},{4,0},{1,5},{5,1},{2,6},{6,2},{3,7},{7,3},{8,12},{12,8},{9,1... | collective-permute-start | bytes 1179656 | tf_op jit(solution)/shard_map/ppermute | solution.py:27
  152.6 20.4 %collective-permute-start.10 = (bf16[256,768]{0,1:T(8,128)(2,1)}, bf16[256,768]{0,1:T(8,128)(2,1)}, u32[]{:S(2)}, u32[]{:S(2)}) collective-permute-start(bf16[256,768]{0,1:T(8,128)(2,1)} %pad_maximum_fusion.5), channel_id=1, source_target_pairs={{0,8},{8,0},{1,9},{9,1},{2,10},{10,2},{3,11},{11,3},{4,12},{12,4},... | collective-permute-start | bytes 1179656 | tf_op jit(solution)/shard_map/ppermute | solution.py:27
  167.6 7.5 %copy-start.11 = (bf16[32,8,48]{2,1,0:T(8,128)(2,1)S(1)}, bf16[32,8,48]{2,1,0:T(8,128)(2,1)}, u32[]{:S(2)}) copy-start(bf16[32,8,48]{2,1,0:T(8,128)(2,1)} %select_reduce_fusion.2) | copy-start | bytes 73732
  167.6 33.3 %collective-permute-start.2 = (bf16[512,768]{0,1:T(8,128)(2,1)}, bf16[512,768]{0,1:T(8,128)(2,1)}, u32[]{:S(2)}, u32[]{:S(2)}) collective-permute-start(bf16[512,768]{0,1:T(8,128)(2,1)} %pad_maximum_fusion.1), channel_id=1, source_target_pairs={{0,4},{4,0},{1,5},{5,1},{2,6},{6,2},{3,7},{7,3},{8,12},{12,8},{9,1... | collective-permute-start | bytes 2359304 | tf_op jit(solution)/shard_map/ppermute | solution.py:27
  171.5 35.5 %collective-permute-start.6 = (bf16[512,768]{0,1:T(8,128)(2,1)}, bf16[512,768]{0,1:T(8,128)(2,1)}, u32[]{:S(2)}, u32[]{:S(2)}) collective-permute-start(bf16[512,768]{0,1:T(8,128)(2,1)} %pad_maximum_fusion.2), channel_id=1, source_target_pairs={{0,8},{8,0},{1,9},{9,1},{2,10},{10,2},{3,11},{11,3},{4,12},{12,4},... | collective-permute-start | bytes 2359304 | tf_op jit(solution)/shard_map/ppermute | solution.py:27
  183.3 19.1 %copy-start.10 = (bf16[128,384]{0,1:T(8,128)(2,1)S(1)}, bf16[128,384]{0,1:T(8,128)(2,1)}, u32[]{:S(2)}) copy-start(bf16[128,384]{0,1:T(8,128)(2,1)} %copy.142) | copy-start | bytes 294916
  207.0 3.8 %copy-start.9 = (bf16[64,8,48]{2,1,0:T(8,128)(2,1)S(1)}, bf16[64,8,48]{2,1,0:T(8,128)(2,1)}, u32[]{:S(2)}) copy-start(bf16[64,8,48]{2,1,0:T(8,128)(2,1)} %select_reduce_fusion.3) | copy-start | bytes 147460
  210.8 1.8 copy-start.1
  212.5 1.5 copy-start.19
  213.6 13.8 %copy-start.7 = (f32[1,128,8,48]{1,3,2,0:T(8,128)S(1)}, f32[1,128,8,48]{1,3,2,0:T(8,128)}, u32[]{:S(2)}) copy-start(f32[1,128,8,48]{1,3,2,0:T(8,128)} %copy.170) | copy-start | bytes 589828
  213.6 15.1 %copy-start.6 = (f32[1,128,8,48]{1,3,2,0:T(8,128)S(1)}, f32[1,128,8,48]{1,3,2,0:T(8,128)}, u32[]{:S(2)}) copy-start(f32[1,128,8,48]{1,3,2,0:T(8,128)} %copy.179) | copy-start | bytes 589828
  216.1 14.0 %copy-start.13 = (f32[128,8]{0,1:T(8,128)S(1)}, f32[128,8]{0,1:T(8,128)}, u32[]{:S(2)}) copy-start(f32[128,8]{0,1:T(8,128)} %copy.184) | copy-start | bytes 12292
  216.1 17.0 %copy-start.29 = (f32[384]{0:T(512)S(1)}, f32[384]{0:T(512)}, u32[]{:S(2)}) copy-start(f32[384]{0:T(512)} %param.51) | copy-start | bytes 4612
  216.3 16.9 %copy-start.8 = (bf16[384,768]{1,0:T(8,128)(2,1)S(1)}, bf16[384,768]{1,0:T(8,128)(2,1)}, u32[]{:S(2)}) copy-start(bf16[384,768]{1,0:T(8,128)(2,1)} %param.52) | copy-start | bytes 1769476
where the time goes:
time: 236 us; the launch traced here: 234 us
  local copies, waits for them, and re-layouts  73.4 us (31%)
  waiting for transfers between devices  57.4 us (24%)
  other arithmetic  48 us (20%)
  starting transfers between devices  35.6 us (15%)
  matrix products  17 us (7%)
  between operations  2.61 us (1%)
    concatenate x15, other arithmetic, local(): current = jnp.concatenate([current, partner], axis=0)  18.8 us
    ppermute x19, waiting for transfers between devices, swapped(): return lax.ppermute(block, axis, route)  17.7 us
    ppermute x19, starting transfers between devices, swapped(): return lax.ppermute(block, axis, route)  17.1 us
    all_to_all x1, waiting for transfers between devices, local(): lax.all_to_all(outbound(tile_heads), 'seq', split_axis=1, concat_axis=1,...  15.7 us
    all_to_all x1, waiting for transfers between devices, local(): lax.all_to_all(outbound(tile_stream), 'seq', split_axis=1, concat_axis=1,...  14.6 us
    reduce_sum x8, other arithmetic, select_heads(): jnp.sum(jnp.where(member, shaped, jnp.zeros((), shaped.dtype)), axis=1)  10.5 us
    concatenate x4, local copies, waits for them, and re-layouts, local(): current = jnp.concatenate([current, partner], axis=0)  10.2 us
    broadcast_in_dim x17, local copies, waits for them, and re-layouts, spread_heads(): jnp.where(member, values[:, None], jnp.asarray(fill_value, values.dtype))  10.2 us
  transfers between devices with their start and end apart: 22, of which 4 were waited for; matrix products, arithmetic and copies ran while one was open for 34% of the time, Pallas kernels for 0%

commit v1 on v0

--- a/solution.py
+++ b/solution.py
@@ -4,6 +4,8 @@
 import jax.numpy as jnp
 import numpy as np
 from jax import lax
+from jax.experimental import pallas as pl
+from jax.experimental.pallas import tpu as pltpu
 from jax.sharding import PartitionSpec as P
 
 HEAD_DIM = 48
@@ -65,7 +67,7 @@
     return placed.reshape((values.shape[0] * stride,) + values.shape[1:])
 
 
-def local(
+def local_general(
     tile_heads,
     tile_stream,
     tissue_counts,
@@ -189,6 +191,378 @@
     return jnp.dot(inner, output_weight, preferred_element_type=jnp.float32).astype(jnp.bfloat16)
 
 
+MESH = pl.DeviceIdType.MESH
+PIECE = 3 * HEAD_DIM
+HALF = 1024
+NT = (((1,), (1,)), ((), ()))
+TN = (((0,), (0,)), ((), ()))
+F32 = jnp.float32
+BF16 = jnp.bfloat16
+MIB = 2**20
+
+
+def encode_kernel(
+    heads_ref,
+    stream_ref,
+    scale_ref,
+    gain_ref,
+    bias_ref,
+    embed_bias_ref,
+    slide_gain_ref,
+    head_weight_hbm,
+    embed_weight_hbm,
+    triple_weight_hbm,
+    recv_ref,
+    head_weight,
+    embed_weight,
+    triple_weight,
+    outbox,
+    load_sem,
+    own_sem,
+    send_sem,
+    pass_sem,
+    recv_sem,
+):
+    group = lax.axis_index("groups")
+    me = lax.axis_index("seq")
+    chip, core = me // 2, lax.rem(me, 2)
+    sibling = 2 * chip + 1 - core
+    chips = HEADS
+    depth = head_weight.shape[0]
+    part = depth // 4
+    loads = [
+        pltpu.make_async_copy(
+            head_weight_hbm.at[pl.ds(i * part, part)],
+            head_weight.at[pl.ds(i * part, part)],
+            load_sem.at[i],
+        )
+        for i in range(4)
+    ]
+    loads.append(pltpu.make_async_copy(embed_weight_hbm, embed_weight, load_sem.at[4]))
+    loads.append(pltpu.make_async_copy(triple_weight_hbm, triple_weight, load_sem.at[5]))
+    for load in loads:
+        load.start()
+
+    barrier = pltpu.get_barrier_semaphore()
+    for off in range(1, chips):
+        peer = 2 * lax.rem(chip + off, chips) + core
+        pl.semaphore_signal(barrier, inc=1, device_id=(group, peer), device_id_type=MESH)
+    pl.semaphore_signal(barrier, inc=1, device_id=(group, sibling), device_id_type=MESH)
+
+    blended = None
+    for i in range(4):
+        loads[i].wait()
+        term = jnp.dot(
+            heads_ref[:, i * part : (i + 1) * part],
+            head_weight[i * part : (i + 1) * part, :],
+            preferred_element_type=F32,
+        )
+        blended = term if blended is None else blended + term
+    summed = stream_ref[...].astype(F32) + scale_ref[...] * blended
+    embedding = (layer_norm(summed, gain_ref[...]) + bias_ref[...]).astype(BF16)
+    loads[4].wait()
+    slide_rows = (
+        jnp.dot(embedding, embed_weight[...], preferred_element_type=F32) + embed_bias_ref[...]
+    ).astype(BF16)
+    normed = layer_norm(slide_rows.astype(F32), slide_gain_ref[...]).astype(BF16)
+    loads[5].wait()
+    triple = jnp.dot(normed, triple_weight[...], preferred_element_type=F32)
+    turned = triple.T.astype(BF16)
+    inner = HEADS * HEAD_DIM
+    for h in range(HEADS):
+        for kind in range(3):
+            low = kind * inner + h * HEAD_DIM
+            outbox[h, kind * HEAD_DIM : (kind + 1) * HEAD_DIM, :] = turned[low : low + HEAD_DIM, :]
+
+    pl.semaphore_wait(barrier, chips)
+    sends = []
+    for off in range(1, chips):
+        to = lax.rem(chip + off, chips)
+        copy = pltpu.make_async_remote_copy(
+            src_ref=outbox.at[to],
+            dst_ref=recv_ref.at[me],
+            send_sem=send_sem.at[off],
+            recv_sem=recv_sem.at[me],
+            device_id=(group, 2 * to + core),
+            device_id_type=MESH,
+        )
+        copy.start()
+        sends.append(copy)
+    copy = pltpu.make_async_remote_copy(
+        src_ref=outbox.at[chip],
+        dst_ref=recv_ref.at[me],
+        send_sem=send_sem.at[0],
+        recv_sem=recv_sem.at[me],
+        device_id=(group, sibling),
+        device_id_type=MESH,
+    )
+    copy.start()
+    sends.append(copy)
+    own = pltpu.make_async_copy(outbox.at[chip], recv_ref.at[me], own_sem)
+    own.start()
+    for off in range(1, chips):
+        source = 2 * lax.rem(chip + chips - off, chips) + core
+        onward = pltpu.make_async_remote_copy(
+            src_ref=recv_ref.at[source],
+            dst_ref=recv_ref.at[source],
+            send_sem=pass_sem.at[off],
+            recv_sem=recv_sem.at[source],
+            device_id=(group, sibling),
+            device_id_type=MESH,
+        )
+        onward.wait_recv()
+        onward.start()
+        sends.append(onward)
+    for off in range(chips):
+        source = 2 * lax.rem(chip + chips - off, chips) + 1 - core
+        pltpu.make_async_remote_copy(
+            src_ref=recv_ref.at[source],
+            dst_ref=recv_ref.at[source],
+            send_sem=pass_sem.at[0],
+            recv_sem=recv_sem.at[source],
+            device_id=(group, sibling),
+            device_id_type=MESH,
+        ).wait_recv()
+    for copy in sends:
+        copy.wait_send()
+    own.wait()
+
+
+def shared_depth(index, shift):
+    residue = (index + 8 - shift) & 7
+    depth = jnp.where(residue & 4 != 0, 3, 4)
+    depth = jnp.where(residue & 2 != 0, 2, depth)
+    return jnp.where(residue & 1 != 0, 1, depth)
+
+
+def attend(keys, queries, multiplicity):
+    scaling = 1.0 / math.sqrt(HEAD_DIM)
+    scores = [
+        lax.dot_general(block, queries, NT, preferred_element_type=F32) for block in keys
+    ]
+    highest = scores[0].max(axis=0, keepdims=True)
+    for block in scores[1:]:
+        highest = jnp.maximum(highest, block.max(axis=0, keepdims=True))
+    total = blended = None
+    for block, values, times in zip(scores, keys, multiplicity):
+        weights = jnp.exp((block - highest) * scaling)
+        if times is not None:
+            weights = weights * times
+        part_total = weights.sum(axis=0, keepdims=True)
+        part = lax.dot_general(values, weights.astype(BF16), TN, preferred_element_type=F32)
+        total = part_total if total is None else total + part_total
+        blended = part if blended is None else blended + part
+    return blended[2 * HEAD_DIM : PIECE, :] / total
+
+
+def attention_kernel(counts_ref, pieces_ref, out_ref, left, right):
+    me = lax.axis_index("seq")
+    head, side = me // 2, lax.rem(me, 2)
+    parity, shift = lax.rem(head, 2), head // 2
+    slots = pieces_ref.shape[2]
+    unit = (
+        lax.broadcasted_iota(jnp.int32, (slots, slots), 0)
+        == lax.broadcasted_iota(jnp.int32, (slots, slots), 1)
+    ).astype(BF16)
+    right[...] = jnp.zeros_like(right)
+    start = 0
+    for d in range(pieces_ref.shape[0]):
+        rows = lax.dot_general(unit, pieces_ref[d], NT, preferred_element_type=F32)
+        left[pl.ds(start, slots), :] = rows[:, :128]
+        right[pl.ds(start, slots), : PIECE - 128] = rows[:, 128:]
+        start = start + counts_ref[d]
+
+    def pick(first, which):
+        place = pl.ds(first + which, HALF // 2, stride=2)
+        return jnp.concatenate(
+            [left[place, :].astype(BF16), right[place, :].astype(BF16)], axis=1
+        )
+
+    def as_queries(rows):
+        lane = lax.broadcasted_iota(jnp.int32, (HALF // 2, 128), 1)
+        kept = jnp.where(lane < HEAD_DIM, rows[:, :128].astype(F32), 0.0)
+        moved = pltpu.roll(kept, HEAD_DIM, 1).astype(BF16)
+        return jnp.concatenate([moved, jnp.zeros_like(moved)], axis=1)
+
+    near = pick(side * HALF, parity)
+    near_off = pick(side * HALF, 1 - parity)
+    far = pick((1 - side) * HALF, parity)
+    count = HALF // 2
+    key_depth = shared_depth(lax.broadcasted_iota(jnp.int32, (count, 1), 0), shift)
+    query_depth = shared_depth(lax.broadcasted_iota(jnp.int32, (1, count), 1), shift)
+    times = jnp.minimum(key_depth, query_depth).astype(F32)
+    same = attend([near, near_off, far], as_queries(near), [times + 1.0, None, times])
+    off = attend([near, near_off], as_queries(near_off), [None, None])
+    even = jnp.where(parity == 0, same, off).astype(BF16)
+    odd = jnp.where(parity == 0, off, same).astype(BF16)
+    for t in range(HALF // TILE_DEV):
+        low = t * (TILE_DEV // 2)
+        out_ref[t] = jnp.concatenate(
+            [even[:, low : low + TILE_DEV // 2], odd[:, low : low + TILE_DEV // 2]], axis=1
+        )
+
+
+def project_kernel(tiles_ref, gain_ref, weight_ref, out_ref, inbox, own_sem, send_sem, recv_sem):
+    group = lax.axis_index("groups")
+    me = lax.axis_index("seq")
+    devices = 2 * HEADS
+    barrier = pltpu.get_barrier_semaphore()
+    for off in range(1, devices):
+        peer = lax.rem(me + off, devices)
+        pl.semaphore_signal(barrier, inc=1, device_id=(group, peer), device_id_type=MESH)
+    pl.semaphore_wait(barrier, devices - 1)
+    head, side = me // 2, lax.rem(me, 2)
+    home_side = me // HEADS
+
+    def remote(t):
+        return pltpu.make_async_remote_copy(
+            src_ref=tiles_ref.at[t],
+            dst_ref=inbox.at[head],
+            send_sem=send_sem.at[t],
+            recv_sem=recv_sem.at[head],
+            device_id=(group, side * HEADS + t),
+            device_id_type=MESH,
+        )
+
+    for t in range(HEADS):
+
+        @pl.when(side * HEADS + t != me)
+        def _():
+            remote(t).start()
+
+        @pl.when(side * HEADS + t == me)
+        def _():
+            own = pltpu.make_async_copy(tiles_ref.at[t], inbox.at[head], own_sem)
+            own.start()
+            own.wait()
+
+    for h in range(HEADS):
+
+        @pl.when(2 * h + home_side != me)
+        def _():
+            pltpu.make_async_remote_copy(
+                src_ref=tiles_ref.at[0],
+                dst_ref=inbox.at[h],
+                send_sem=send_sem.at[0],
+                recv_sem=recv_sem.at[h],
+                device_id=(group, 2 * h + home_side),
+                device_id_type=MESH,
+            ).wait_recv()
+
+    mixed = inbox[...].astype(F32).reshape(HEADS * HEAD_DIM, TILE_DEV)
+    average = jnp.mean(mixed, axis=0, keepdims=True)
+    centred = mixed - average
+    spread = jnp.mean(centred * centred, axis=0, keepdims=True)
+    inner = (centred * lax.rsqrt(spread + EPSILON) * gain_ref[...]).astype(BF16)
+    row = lax.broadcasted_iota(jnp.int32, (TILE_DEV, TILE_DEV), 0)
+    lane = lax.broadcasted_iota(jnp.int32, (TILE_DEV, TILE_DEV), 1)
+    half = TILE_DEV // 2
+    order = (row == 2 * lax.rem(lane, half) + lane // half).astype(BF16)
+    rows = lax.dot_general(order, inner, NT, preferred_element_type=F32).astype(BF16)
+    out_ref[...] = jnp.dot(rows, weight_ref[...], preferred_element_type=F32).astype(BF16)
+    for t in range(HEADS):
+
+        @pl.when(side * HEADS + t != me)
+        def _():
+            remote(t).wait_send()
+
+
+def local(
+    tile_heads,
+    tile_stream,
+    tissue_counts,
+    head_weight,
+    stream_scale,
+    final_gain,
+    final_bias,
+    embed_weight,
+    embed_bias,
+    slide_gain,
+    triple_weight,
+    inner_gain,
+    output_weight,
+):
+    devices = lax.axis_size("seq")
+    if devices != 2 * HEADS:
+        return local_general(
+            tile_heads,
+            tile_stream,
+            tissue_counts,
+            head_weight,
+            stream_scale,
+            final_gain,
+            final_bias,
+            embed_weight,
+            embed_bias,
+            slide_gain,
+            triple_weight,
+            inner_gain,
+            output_weight,
+        )
+    slots = tile_heads.shape[0]
+    vmem = pl.BlockSpec(memory_space=pltpu.VMEM)
+    smem = pl.BlockSpec(memory_space=pltpu.SMEM)
+    hbm = pl.BlockSpec(memory_space=pl.ANY)
+    dma = pltpu.SemaphoreType.DMA
+    pieces = pl.pallas_call(
+        encode_kernel,
+        out_shape=jax.ShapeDtypeStruct((devices, PIECE, slots), BF16),
+        in_specs=[vmem] * 7 + [hbm] * 3,
+        out_specs=hbm,
+        scratch_shapes=[
+            pltpu.VMEM(head_weight.shape, BF16),
+            pltpu.VMEM(embed_weight.shape, BF16),
+            pltpu.VMEM(triple_weight.shape, BF16),
+            pltpu.VMEM((HEADS, PIECE, slots), BF16),
+            dma((6,)),
+            dma,
+            dma((HEADS,)),
+            dma((HEADS,)),
+            dma((devices,)),
+        ],
+        compiler_params=pltpu.CompilerParams(
+            collective_id=0, has_side_effects=True, vmem_limit_bytes=40 * MIB
+        ),
+    )(
+        tile_heads,
+        tile_stream,
+        stream_scale[None],
+        final_gain[None],
+        final_bias[None],
+        embed_bias[None],
+        slide_gain[None],
+        head_weight,
+        embed_weight,
+        triple_weight,
+    )
+    tiles = pl.pallas_call(
+        attention_kernel,
+        out_shape=jax.ShapeDtypeStruct((HEADS, HEAD_DIM, TILE_DEV), BF16),
+        in_specs=[smem, vmem],
+        out_specs=vmem,
+        scratch_shapes=[
+            pltpu.VMEM((2 * HALF + slots, 128), F32),
+            pltpu.VMEM((2 * HALF + slots, 128), F32),
+        ],
+        compiler_params=pltpu.CompilerParams(vmem_limit_bytes=40 * MIB),
+    )(tissue_counts, pieces)
+    return pl.pallas_call(
+        project_kernel,
+        out_shape=jax.ShapeDtypeStruct((TILE_DEV, output_weight.shape[1]), BF16),
+        in_specs=[vmem] * 3,
+        out_specs=vmem,
+        scratch_shapes=[
+            pltpu.VMEM((HEADS, HEAD_DIM, TILE_DEV), BF16),
+            dma,
+            dma((HEADS,)),
+            dma((HEADS,)),
+        ],
+        compiler_params=pltpu.CompilerParams(
+            collective_id=1, has_side_effects=True, vmem_limit_bytes=16 * MIB
+        ),
+    )(tiles, inner_gain[:, None], output_weight)
+
+
 def solution(mesh):
     placed = (
         P(("groups", "seq"), None),

time: 236 us -> 48.7 us (0.21)
  local copies, waits for them, and re-layouts: 73.4 us -> 12 us
  waiting for transfers between devices: 57.4 us -> 0 us
  other arithmetic: 48 us -> 0 us
  Pallas kernels: 0 us -> 36.1 us
  starting transfers between devices: 35.6 us -> 0 us
  matrix products: 17 us -> 0 us
  between operations: 2.61 us -> 0.07 us
    all_to_all x3 -> x0, waiting for transfers between devices: 39.7 us -> none  [the longest x1 15.7 us: local(): lax.all_to_all(outbound(tile_heads), 'seq', split_axis=1, concat_axis=1,...]
    pallas_call x0 -> x3, Pallas kernels: none -> 36.1 us  [the longest x1 22.3 us: local(): pl.pallas_call(encode_kernel, out_shape=jax.ShapeDtypeStruct((devices, PI...]
    concatenate x18 -> x0, other arithmetic: 22.9 us -> none  [the longest x15 18.8 us: local(): current = jnp.concatenate([current, partner], axis=0)]
    all_to_all x3 -> x0, starting transfers between devices: 18.5 us -> none  [the longest x1 7.5 us: local(): lax.all_to_all(outbound(tile_heads), 'seq', split_axis=1, concat_axis=1,...]
    ppermute x19 -> x0, waiting for transfers between devices: 17.7 us -> none  [swapped(): return lax.ppermute(block, axis, route)]
    ppermute x19 -> x0, starting transfers between devices: 17.1 us -> none  [swapped(): return lax.ppermute(block, axis, route)]
    dot_general x14 -> x0, matrix products: 17 us -> none  [the longest x5 6.12 us: local(): jnp.einsum('qhd,khd->hqk', own_queries, gathered_rows[:, :, :HEAD_DIM], p...]
    concatenate x12 -> x0, local copies, waits for them, and re-layouts: 16.3 us -> none  [the longest x4 10.2 us: local(): current = jnp.concatenate([current, partner], axis=0)]
  transfers between devices with their start and end apart: 22 -> 0, of which waited for: 4 -> 0; matrix products, arithmetic and copies ran while one was open for 34% -> 0% of each run, Pallas kernels for 0% -> 0%
where the time goes in v1:
time: 48.7 us; the launch traced here: 48.2 us
  Pallas kernels  36.1 us (74%)
  local copies, waits for them, and re-layouts  12 us (25%)
    pallas_call x1, Pallas kernels, local(): pl.pallas_call(encode_kernel, out_shape=jax.ShapeDtypeStruct((devices, PI...  22.3 us
    pallas_call x1, Pallas kernels, local(): pl.pallas_call(project_kernel, out_shape=jax.ShapeDtypeStruct((TILE_DEV,...  9.4 us
    unnamed x17, local copies, waits for them, and re-layouts  8.43 us
    pallas_call x1, Pallas kernels, local(): pl.pallas_call(attention_kernel, out_shape=jax.ShapeDtypeStruct((HEADS, H...  4.46 us

profile of v1, /device:TPU:0, one launch (start us, length us, event | category | flops | bytes accessed | tf_op | source)
XLA Modules:
  0.0 48.2 jit_solution(4571242233481145493)
XLA Ops:
  0.0 0.7 %broadcast_in_dim.18.scale_ref = f32[1,1536]{1,0:T(1,128)S(1)} reshape(f32[1536]{0:T(1024)} %param.17) | data formatting | bytes 12288 | tf_op jit(solution)/shard_map/broadcast_in_dim | solution.py:529
  0.7 0.7 %broadcast_in_dim.19.gain_ref = f32[1,1536]{1,0:T(1,128)S(1)} reshape(f32[1536]{0:T(1024)} %param.18) | data formatting | bytes 12288 | tf_op jit(solution)/shard_map/broadcast_in_dim | solution.py:530
  1.4 0.7 %broadcast_in_dim.20.bias_ref = f32[1,1536]{1,0:T(1,128)S(1)} reshape(f32[1536]{0:T(1024)} %param.19) | data formatting | bytes 12288 | tf_op jit(solution)/shard_map/broadcast_in_dim | solution.py:531
  2.1 0.7 %broadcast_in_dim.21.embed_bias_ref = f32[1,768]{1,0:T(1,128)S(1)} reshape(f32[768]{0:T(1024)} %param.21) | data formatting | bytes 6144 | tf_op jit(solution)/shard_map/broadcast_in_dim | solution.py:532
  2.8 0.7 %broadcast_in_dim.22.slide_gain_ref = f32[1,768]{1,0:T(1,128)S(1)} reshape(f32[768]{0:T(1024)} %param.22) | data formatting | bytes 6144 | tf_op jit(solution)/shard_map/broadcast_in_dim | solution.py:533
  3.5 0.0 copy-start
  3.5 2.3 %copy-done = bf16[1536,1536]{1,0:T(8,128)(2,1)S(1)} copy-done((bf16[1536,1536]{1,0:T(8,128)(2,1)S(1)}, bf16[1536,1536]{1,0:T(8,128)(2,1)}, u32[]{:S(2)}) %copy-start) | copy-done | bytes 4718616
  5.8 0.0 copy-start.1
  5.8 1.7 %copy-done.1 = bf16[1536,768]{1,0:T(8,128)(2,1)S(1)} copy-done((bf16[1536,768]{1,0:T(8,128)(2,1)S(1)}, bf16[1536,768]{1,0:T(8,128)(2,1)}, u32[]{:S(2)}) %copy-start.1) | copy-done | bytes 2359320
  7.5 0.0 copy-start.2
  7.5 1.5 %copy-done.2 = bf16[768,1152]{1,0:T(8,128)(2,1)S(1)} copy-done((bf16[768,1152]{1,0:T(8,128)(2,1)S(1)}, bf16[768,1152]{1,0:T(8,128)(2,1)}, u32[]{:S(2)}) %copy-start.2) | copy-done | bytes 1769496
  9.0 0.0 copy-start.3
  9.0 1.1 %copy-done.3 = bf16[256,1536]{1,0:T(8,128)(2,1)S(1)} copy-done((bf16[256,1536]{1,0:T(8,128)(2,1)S(1)}, bf16[256,1536]{1,0:T(8,128)(2,1)}, u32[]{:S(2)}) %copy-start.3) | copy-done | bytes 786456
  10.1 0.0 copy-start.4
  10.1 1.1 %copy-done.4 = bf16[256,1536]{1,0:T(8,128)(2,1)S(1)} copy-done((bf16[256,1536]{1,0:T(8,128)(2,1)S(1)}, bf16[256,1536]{1,0:T(8,128)(2,1)}, u32[]{:S(2)}) %copy-start.4) | copy-done | bytes 786456
  11.2 0.0 copy-start.6
  11.2 0.0 copy-start.7
  11.2 0.0 copy-start.5
  11.2 22.3 %shard_map.127.pieces_ref = bf16[16,144,256]{2,1,0:T(8,128)(2,1)S(1)} custom-call(bf16[256,1536]{1,0:T(8,128)(2,1)S(1)} %copy-done.3, bf16[256,1536]{1,0:T(8,128)(2,1)S(1)} %copy-done.4, f32[1,1536]{1,0:T(1,128)S(1)} %broadcast_in_dim.18.scale_ref, f32[1,1536]{1,0:T(1,128)S(1)} %broadcast_in_dim.19.gain_ref, f32[1,1536]{1,0:T(1,128)S(1)} %broadcast_in_dim.20.bias_ref, ...), custom_call_target="tpu_custom_call" | custom-call | tf_op jit(solution)/shard_map/pallas_call | solution.py:507
  33.5 0.0 copy-done.6
  33.5 4.5 %shard_map.128.tiles_ref = bf16[8,48,128]{2,1,0:T(8,128)(2,1)S(1)} custom-call(s32[16]{0:T(128)S(1)} %copy-done.6, bf16[16,144,256]{2,1,0:T(8,128)(2,1)S(1)} %shard_map.127.pieces_ref), custom_call_target="tpu_custom_call" | custom-call | tf_op jit(solution)/shard_map/pallas_call | solution.py:538
  38.0 0.0 copy-done.7
  38.0 0.1 broadcast_in_dim.24.gain_ref
  38.1 0.0 copy-done.5
  38.1 9.4 %shard_map.129 = bf16[128,768]{1,0:T(8,128)(2,1)S(1)} custom-call(bf16[8,48,128]{2,1,0:T(8,128)(2,1)S(1)} %shard_map.128.tiles_ref, f32[384,1]{1,0:T(8,128)S(1)} %broadcast_in_dim.24.gain_ref, bf16[384,768]{1,0:T(8,128)(2,1)S(1)} %copy-done.5), custom_call_target="tpu_custom_call" | custom-call | tf_op jit(solution)/shard_map/pallas_call | solution.py:549
  47.5 0.7 %copy.16 = bf16[128,768]{1,0:T(8,128)(2,1)} copy(bf16[128,768]{1,0:T(8,128)(2,1)S(1)} %shard_map.129) | data formatting | bytes 393216
Async XLA Ops:
  3.5 2.3 %copy-start = (bf16[1536,1536]{1,0:T(8,128)(2,1)S(1)}, bf16[1536,1536]{1,0:T(8,128)(2,1)}, u32[]{:S(2)}) copy-start(bf16[1536,1536]{1,0:T(8,128)(2,1)} %head_weight_hbm.1) | copy-start | bytes 14155780
  5.8 1.7 %copy-start.1 = (bf16[1536,768]{1,0:T(8,128)(2,1)S(1)}, bf16[1536,768]{1,0:T(8,128)(2,1)}, u32[]{:S(2)}) copy-start(bf16[1536,768]{1,0:T(8,128)(2,1)} %embed_weight_hbm.1) | copy-start | bytes 7077892
  7.5 1.5 %copy-start.2 = (bf16[768,1152]{1,0:T(8,128)(2,1)S(1)}, bf16[768,1152]{1,0:T(8,128)(2,1)}, u32[]{:S(2)}) copy-start(bf16[768,1152]{1,0:T(8,128)(2,1)} %triple_weight_hbm.1) | copy-start | bytes 5308420
  9.0 1.1 %copy-start.3 = (bf16[256,1536]{1,0:T(8,128)(2,1)S(1)}, bf16[256,1536]{1,0:T(8,128)(2,1)}, u32[]{:S(2)}) copy-start(bf16[256,1536]{1,0:T(8,128)(2,1)} %heads_ref.1) | copy-start | bytes 2359300
  10.1 1.1 %copy-start.4 = (bf16[256,1536]{1,0:T(8,128)(2,1)S(1)}, bf16[256,1536]{1,0:T(8,128)(2,1)}, u32[]{:S(2)}) copy-start(bf16[256,1536]{1,0:T(8,128)(2,1)} %stream_ref.1) | copy-start | bytes 2359300
  11.2 22.3 %copy-start.6 = (s32[16]{0:T(128)S(1)}, s32[16]{0:T(128)}, u32[]{:S(2)}) copy-start(s32[16]{0:T(128)} %counts_ref.1) | copy-start | bytes 196
  11.2 26.8 %copy-start.7 = (f32[384]{0:T(512)S(1)}, f32[384]{0:T(512)}, u32[]{:S(2)}) copy-start(f32[384]{0:T(512)} %param.24) | copy-start | bytes 4612
  11.2 26.9 %copy-start.5 = (bf16[384,768]{1,0:T(8,128)(2,1)S(1)}, bf16[384,768]{1,0:T(8,128)(2,1)}, u32[]{:S(2)}) copy-start(bf16[384,768]{1,0:T(8,128)(2,1)} %weight_ref.1) | copy-start | bytes 1769476

commit v2 on v1

--- a/solution.py
+++ b/solution.py
@@ -201,9 +201,13 @@
 MIB = 2**20
 
 
+ROUTE = (4, 3, 5, 2, 6, 1, 7)
+HALVES = 2
+
+
 def encode_kernel(
-    heads_ref,
-    stream_ref,
+    heads_hbm,
+    stream_hbm,
     scale_ref,
     gain_ref,
     bias_ref,
@@ -213,6 +217,8 @@
     embed_weight_hbm,
     triple_weight_hbm,
     recv_ref,
+    heads,
+    stream,
     head_weight,
     embed_weight,
     triple_weight,
@@ -230,18 +236,24 @@
     chips = HEADS
     depth = head_weight.shape[0]
     part = depth // 4
-    loads = [
-        pltpu.make_async_copy(
-            head_weight_hbm.at[pl.ds(i * part, part)],
-            head_weight.at[pl.ds(i * part, part)],
-            load_sem.at[i],
-        )
-        for i in range(4)
+    rows = heads.shape[0] // HALVES
+
+    def load(source, target, first, count, sem):
+        copy = pltpu.make_async_copy(
+            source.at[pl.ds(first, count)], target.at[pl.ds(first, count)], load_sem.at[sem]
+        )
+        copy.start()
+        return copy
+
+    head_loads = [load(heads_hbm, heads, 0, rows, 0)]
+    weight_loads = [
+        load(head_weight_hbm, head_weight, i * part, part, 1 + i) for i in range(4)
     ]
-    loads.append(pltpu.make_async_copy(embed_weight_hbm, embed_weight, load_sem.at[4]))
-    loads.append(pltpu.make_async_copy(triple_weight_hbm, triple_weight, load_sem.at[5]))
-    for load in loads:
-        load.start()
+    stream_loads = [load(stream_hbm, stream, 0, rows, 5)]
+    embed_load = load(embed_weight_hbm, embed_weight, 0, embed_weight.shape[0], 6)
+    triple_load = load(triple_weight_hbm, triple_weight, 0, triple_weight.shape[0], 7)
+    head_loads.append(load(heads_hbm, heads, rows, rows, 8))
+    stream_loads.append(load(stream_hbm, stream, rows, rows, 9))
 
     barrier = pltpu.get_barrier_semaphore()
     for off in range(1, chips):
@@ -249,83 +261,91 @@
         pl.semaphore_signal(barrier, inc=1, device_id=(group, peer), device_id_type=MESH)
     pl.semaphore_signal(barrier, inc=1, device_id=(group, sibling), device_id_type=MESH)
 
-    blended = None
-    for i in range(4):
-        loads[i].wait()
-        term = jnp.dot(
-            heads_ref[:, i * part : (i + 1) * part],
-            head_weight[i * part : (i + 1) * part, :],
-            preferred_element_type=F32,
-        )
-        blended = term if blended is None else blended + term
-    summed = stream_ref[...].astype(F32) + scale_ref[...] * blended
-    embedding = (layer_norm(summed, gain_ref[...]) + bias_ref[...]).astype(BF16)
-    loads[4].wait()
-    slide_rows = (
-        jnp.dot(embedding, embed_weight[...], preferred_element_type=F32) + embed_bias_ref[...]
-    ).astype(BF16)
-    normed = layer_norm(slide_rows.astype(F32), slide_gain_ref[...]).astype(BF16)
-    loads[5].wait()
-    triple = jnp.dot(normed, triple_weight[...], preferred_element_type=F32)
-    turned = triple.T.astype(BF16)
     inner = HEADS * HEAD_DIM
-    for h in range(HEADS):
-        for kind in range(3):
-            low = kind * inner + h * HEAD_DIM
-            outbox[h, kind * HEAD_DIM : (kind + 1) * HEAD_DIM, :] = turned[low : low + HEAD_DIM, :]
-
-    pl.semaphore_wait(barrier, chips)
+    scale = scale_ref[...].reshape(1, -1)
+    gain = gain_ref[...].reshape(1, -1)
+    bias = bias_ref[...].reshape(1, -1)
+    embed_bias = embed_bias_ref[...].reshape(1, -1)
+    slide_gain = slide_gain_ref[...].reshape(1, -1)
     sends = []
-    for off in range(1, chips):
-        to = lax.rem(chip + off, chips)
-        copy = pltpu.make_async_remote_copy(
-            src_ref=outbox.at[to],
-            dst_ref=recv_ref.at[me],
-            send_sem=send_sem.at[off],
-            recv_sem=recv_sem.at[me],
-            device_id=(group, 2 * to + core),
-            device_id_type=MESH,
-        )
-        copy.start()
-        sends.append(copy)
-    copy = pltpu.make_async_remote_copy(
-        src_ref=outbox.at[chip],
-        dst_ref=recv_ref.at[me],
-        send_sem=send_sem.at[0],
-        recv_sem=recv_sem.at[me],
-        device_id=(group, sibling),
-        device_id_type=MESH,
-    )
-    copy.start()
-    sends.append(copy)
-    own = pltpu.make_async_copy(outbox.at[chip], recv_ref.at[me], own_sem)
-    own.start()
-    for off in range(1, chips):
-        source = 2 * lax.rem(chip + chips - off, chips) + core
-        onward = pltpu.make_async_remote_copy(
-            src_ref=recv_ref.at[source],
-            dst_ref=recv_ref.at[source],
-            send_sem=pass_sem.at[off],
-            recv_sem=recv_sem.at[source],
+    owns = []
+    for half in range(HALVES):
+        low = half * rows
+        head_loads[half].wait()
+        blended = None
+        for i in range(4):
+            if half == 0:
+                weight_loads[i].wait()
+            term = jnp.dot(
+                heads[low : low + rows, i * part : (i + 1) * part],
+                head_weight[i * part : (i + 1) * part, :],
+                preferred_element_type=F32,
+            )
+            blended = term if blended is None else blended + term
+        stream_loads[half].wait()
+        summed = stream[low : low + rows, :].astype(F32) + scale * blended
+        embedding = (layer_norm(summed, gain) + bias).astype(BF16)
+        if half == 0:
+            embed_load.wait()
+        slide_rows = (
+            jnp.dot(embedding, embed_weight[...], preferred_element_type=F32) + embed_bias
+        ).astype(BF16)
+        normed = layer_norm(slide_rows.astype(F32), slide_gain).astype(BF16)
+        if half == 0:
+            triple_load.wait()
+        triple = jnp.dot(normed, triple_weight[...], preferred_element_type=F32)
+        turned = triple.T.astype(BF16)
+        for h in range(HEADS):
+            for kind in range(3):
+                first = kind * inner + h * HEAD_DIM
+                outbox[half, h, kind * HEAD_DIM : (kind + 1) * HEAD_DIM, :] = turned[
+                    first : first + HEAD_DIM, :
+                ]
+        if half == 0:
+            pl.semaphore_wait(barrier, chips)
+        for off in ROUTE + (0,):
+            to = lax.rem(chip + off, chips)
+            copy = pltpu.make_async_remote_copy(
+                src_ref=outbox.at[half, to],
+                dst_ref=recv_ref.at[me, half],
+                send_sem=send_sem.at[half, off],
+                recv_sem=recv_sem.at[me, half],
+                device_id=(group, 2 * to + core if off else sibling),
+                device_id_type=MESH,
+            )
+            copy.start()
+            sends.append(copy)
+        own = pltpu.make_async_copy(
+            outbox.at[half, chip], recv_ref.at[me, half], own_sem.at[half]
+        )
+        own.start()
+        owns.append(own)
+
+    def arrival(source, half, sem):
+        return pltpu.make_async_remote_copy(
+            src_ref=recv_ref.at[source, half],
+            dst_ref=recv_ref.at[source, half],
+            send_sem=sem,
+            recv_sem=recv_sem.at[source, half],
             device_id=(group, sibling),
             device_id_type=MESH,
         )
-        onward.wait_recv()
-        onward.start()
-        sends.append(onward)
-    for off in range(chips):
-        source = 2 * lax.rem(chip + chips - off, chips) + 1 - core
-        pltpu.make_async_remote_copy(
-            src_ref=recv_ref.at[source],
-            dst_ref=recv_ref.at[source],
-            send_sem=pass_sem.at[0],
-            recv_sem=recv_sem.at[source],
-            device_id=(group, sibling),
-            device_id_type=MESH,
-        ).wait_recv()
+
+    for half in range(HALVES):
+        for off in ROUTE:
+            source = 2 * lax.rem(chip + chips - off, chips) + core
+            onward = arrival(source, half, pass_sem.at[half, off])
+            onward.wait_recv()
+            onward.start()
+            sends.append(onward)
+    for half in range(HALVES):
+        for off in range(chips):
+            source = 2 * lax.rem(chip + chips - off, chips) + 1 - core
+            arrival(source, half, pass_sem.at[half, 0]).wait_recv()
     for copy in sends:
         copy.wait_send()
-    own.wait()
+    for own in owns:
+        own.wait()
 
 
 def shared_depth(index, shift):
@@ -359,7 +379,7 @@
     me = lax.axis_index("seq")
     head, side = me // 2, lax.rem(me, 2)
     parity, shift = lax.rem(head, 2), head // 2
-    slots = pieces_ref.shape[2]
+    slots = pieces_ref.shape[1] * pieces_ref.shape[3]
     unit = (
         lax.broadcasted_iota(jnp.int32, (slots, slots), 0)
         == lax.broadcasted_iota(jnp.int32, (slots, slots), 1)
@@ -367,7 +387,8 @@
     right[...] = jnp.zeros_like(right)
     start = 0
     for d in range(pieces_ref.shape[0]):
-        rows = lax.dot_general(unit, pieces_ref[d], NT, preferred_element_type=F32)
+        block = jnp.concatenate([pieces_ref[d, half] for half in range(HALVES)], axis=1)
+        rows = lax.dot_general(unit, block, NT, preferred_element_type=F32)
         left[pl.ds(start, slots), :] = rows[:, :128]
         right[pl.ds(start, slots), : PIECE - 128] = rows[:, 128:]
         start = start + counts_ref[d]
@@ -405,14 +426,18 @@
 def project_kernel(tiles_ref, gain_ref, weight_ref, out_ref, inbox, own_sem, send_sem, recv_sem):
     group = lax.axis_index("groups")
     me = lax.axis_index("seq")
-    devices = 2 * HEADS
-    barrier = pltpu.get_barrier_semaphore()
-    for off in range(1, devices):
-        peer = lax.rem(me + off, devices)
-        pl.semaphore_signal(barrier, inc=1, device_id=(group, peer), device_id_type=MESH)
-    pl.semaphore_wait(barrier, devices - 1)
     head, side = me // 2, lax.rem(me, 2)
     home_side = me // HEADS
+    barrier = pltpu.get_barrier_semaphore()
+    for h in range(HEADS):
+
+        @pl.when(2 * h + home_side != me)
+        def _():
+            pl.semaphore_signal(
+                barrier, inc=1, device_id=(group, 2 * h + home_side), device_id_type=MESH
+            )
+
+    pl.semaphore_wait(barrier, HEADS - jnp.where(side == home_side, 1, 0))
 
     def remote(t):
         return pltpu.make_async_remote_copy(
@@ -506,31 +531,33 @@
     dma = pltpu.SemaphoreType.DMA
     pieces = pl.pallas_call(
         encode_kernel,
-        out_shape=jax.ShapeDtypeStruct((devices, PIECE, slots), BF16),
-        in_specs=[vmem] * 7 + [hbm] * 3,
-        out_specs=hbm,
+        out_shape=jax.ShapeDtypeStruct((devices, HALVES, PIECE, slots // HALVES), BF16),
+        in_specs=[hbm] * 2 + [vmem] * 5 + [hbm] * 3,
+        out_specs=vmem,
         scratch_shapes=[
+            pltpu.VMEM(tile_heads.shape, BF16),
+            pltpu.VMEM(tile_stream.shape, BF16),
             pltpu.VMEM(head_weight.shape, BF16),
             pltpu.VMEM(embed_weight.shape, BF16),
             pltpu.VMEM(triple_weight.shape, BF16),
-            pltpu.VMEM((HEADS, PIECE, slots), BF16),
-            dma((6,)),
-            dma,
-            dma((HEADS,)),
-            dma((HEADS,)),
-            dma((devices,)),
+            pltpu.VMEM((HALVES, HEADS, PIECE, slots // HALVES), BF16),
+            dma((10,)),
+            dma((HALVES,)),
+            dma((HALVES, HEADS)),
+            dma((HALVES, HEADS)),
+            dma((devices, HALVES)),
         ],
         compiler_params=pltpu.CompilerParams(
-            collective_id=0, has_side_effects=True, vmem_limit_bytes=40 * MIB
+            collective_id=0, has_side_effects=True, vmem_limit_bytes=56 * MIB
         ),
     )(
         tile_heads,
         tile_stream,
-        stream_scale[None],
-        final_gain[None],
-        final_bias[None],
-        embed_bias[None],
-        slide_gain[None],
+        stream_scale,
+        final_gain,
+        final_bias,
+        embed_bias,
+        slide_gain,
         head_weight,
         embed_weight,
         triple_weight,

time: 48.7 us -> 40 us (0.82)
  local copies, waits for them, and re-layouts: 12 us -> 2.06 us
  Pallas kernels: 36.1 us -> 37.7 us
    unnamed x17 -> x9, local copies, waits for them, and re-layouts: 8.43 us -> 1.95 us
    pallas_call x1, Pallas kernels: 22.3 us -> 25.9 us  [local(): pl.pallas_call(encode_kernel, out_shape=jax.ShapeDtypeStruct((devices, HA...]
    broadcast_in_dim x5 -> x0, local copies, waits for them, and re-layouts: 3.48 us -> none  [the longest x1 0.7 us: local(): stream_scale[None]]
    pallas_call x1, Pallas kernels: 9.4 us -> 7.36 us  [local(): pl.pallas_call(project_kernel, out_shape=jax.ShapeDtypeStruct((TILE_DEV,...]
where the time goes in v2:
time: 40 us; the launch traced here: 39.8 us
  Pallas kernels  37.7 us (94%)
  local copies, waits for them, and re-layouts  2.06 us (5%)
    pallas_call x1, Pallas kernels, local(): pl.pallas_call(encode_kernel, out_shape=jax.ShapeDtypeStruct((devices, HA...  25.9 us
    pallas_call x1, Pallas kernels, local(): pl.pallas_call(project_kernel, out_shape=jax.ShapeDtypeStruct((TILE_DEV,...  7.36 us
    pallas_call x1, Pallas kernels, local(): pl.pallas_call(attention_kernel, out_shape=jax.ShapeDtypeStruct((HEADS, H...  4.48 us
    unnamed x9, local copies, waits for them, and re-layouts  1.95 us

profile of v2, /device:TPU:0, one launch (start us, length us, event | category | flops | bytes accessed | tf_op | source)
XLA Modules:
  0.0 39.8 jit_solution(14464313822841427846)
XLA Ops:
  0.0 0.0 copy-start.2
  0.0 0.0 copy-start.3
  0.0 0.0 copy-start.1
  0.0 25.9 %shard_map.127.pieces_ref = bf16[16,2,144,128]{3,2,1,0:T(8,128)(2,1)} custom-call(bf16[256,1536]{1,0:T(8,128)(2,1)} %heads_hbm.1, bf16[256,1536]{1,0:T(8,128)(2,1)} %stream_hbm.1, f32[1536]{0:T(1024)} %scale_ref.1, f32[1536]{0:T(1024)} %gain_ref.1, f32[1536]{0:T(1024)} %bias_ref.1, f32[768]{0:T(1024)} %embed_bias_ref.1, f32[768]{0:T(1024)} %slide_gain_ref.1, ...), custom_call_target="tpu_custom_call" | custom-call | tf_op jit(solution)/shard_map/pallas_call | solution.py:532
  25.9 0.0 copy-done.2
  25.9 0.0 copy-start
  25.9 1.3 %copy-done = bf16[16,2,144,128]{3,2,1,0:T(8,128)(2,1)S(1)} copy-done((bf16[16,2,144,128]{3,2,1,0:T(8,128)(2,1)S(1)}, bf16[16,2,144,128]{3,2,1,0:T(8,128)(2,1)}, u32[]{:S(2)}) %copy-start) | copy-done | bytes 1179672
  27.2 4.5 %shard_map.128.tiles_ref = bf16[8,48,128]{2,1,0:T(8,128)(2,1)S(1)} custom-call(s32[16]{0:T(128)S(1)} %copy-done.2, bf16[16,2,144,128]{3,2,1,0:T(8,128)(2,1)S(1)} %copy-done), custom_call_target="tpu_custom_call" | custom-call | tf_op jit(solution)/shard_map/pallas_call | solution.py:565
  31.6 0.0 copy-done.3
  31.7 0.1 broadcast_in_dim.4.gain_ref
  31.8 0.0 copy-done.1
  31.8 7.4 %shard_map.129 = bf16[128,768]{1,0:T(8,128)(2,1)S(1)} custom-call(bf16[8,48,128]{2,1,0:T(8,128)(2,1)S(1)} %shard_map.128.tiles_ref, f32[384,1]{1,0:T(8,128)S(1)} %broadcast_in_dim.4.gain_ref, bf16[384,768]{1,0:T(8,128)(2,1)S(1)} %copy-done.1), custom_call_target="tpu_custom_call" | custom-call | tf_op jit(solution)/shard_map/pallas_call | solution.py:576
  39.1 0.7 %copy.16 = bf16[128,768]{1,0:T(8,128)(2,1)} copy(bf16[128,768]{1,0:T(8,128)(2,1)S(1)} %shard_map.129) | data formatting | bytes 393216
Async XLA Ops:
  0.0 25.9 %copy-start.2 = (s32[16]{0:T(128)S(1)}, s32[16]{0:T(128)}, u32[]{:S(2)}) copy-start(s32[16]{0:T(128)} %counts_ref.1) | copy-start | bytes 196
  0.0 31.6 %copy-start.3 = (f32[384]{0:T(512)S(1)}, f32[384]{0:T(512)}, u32[]{:S(2)}) copy-start(f32[384]{0:T(512)} %param.24) | copy-start | bytes 4612
  0.0 31.8 %copy-start.1 = (bf16[384,768]{1,0:T(8,128)(2,1)S(1)}, bf16[384,768]{1,0:T(8,128)(2,1)}, u32[]{:S(2)}) copy-start(bf16[384,768]{1,0:T(8,128)(2,1)} %weight_ref.1) | copy-start | bytes 1769476
  25.9 1.3 %copy-start = (bf16[16,2,144,128]{3,2,1,0:T(8,128)(2,1)S(1)}, bf16[16,2,144,128]{3,2,1,0:T(8,128)(2,1)}, u32[]{:S(2)}) copy-start(bf16[16,2,144,128]{3,2,1,0:T(8,128)(2,1)} %shard_map.127.pieces_ref) | copy-start | bytes 3538948

commit v3 on v2

--- a/solution.py
+++ b/solution.py
@@ -375,39 +375,69 @@
     return blended[2 * HEAD_DIM : PIECE, :] / total
 
 
-def attention_kernel(counts_ref, pieces_ref, out_ref, left, right):
+def compact_kernel(counts_ref, pieces, near_ref, off_ref, far_ref, left, right):
     me = lax.axis_index("seq")
     head, side = me // 2, lax.rem(me, 2)
-    parity, shift = lax.rem(head, 2), head // 2
-    slots = pieces_ref.shape[1] * pieces_ref.shape[3]
+    parity = lax.rem(head, 2)
+    slots = pieces.shape[1] * pieces.shape[3]
     unit = (
         lax.broadcasted_iota(jnp.int32, (slots, slots), 0)
         == lax.broadcasted_iota(jnp.int32, (slots, slots), 1)
     ).astype(BF16)
     right[...] = jnp.zeros_like(right)
     start = 0
-    for d in range(pieces_ref.shape[0]):
-        block = jnp.concatenate([pieces_ref[d, half] for half in range(HALVES)], axis=1)
+    for d in range(pieces.shape[0]):
+        block = jnp.concatenate([pieces[d, half] for half in range(HALVES)], axis=1)
         rows = lax.dot_general(unit, block, NT, preferred_element_type=F32)
         left[pl.ds(start, slots), :] = rows[:, :128]
         right[pl.ds(start, slots), : PIECE - 128] = rows[:, 128:]
         start = start + counts_ref[d]
 
-    def pick(first, which):
+    def pick(target, first, which):
         place = pl.ds(first + which, HALF // 2, stride=2)
-        return jnp.concatenate(
-            [left[place, :].astype(BF16), right[place, :].astype(BF16)], axis=1
-        )
-
-    def as_queries(rows):
-        lane = lax.broadcasted_iota(jnp.int32, (HALF // 2, 128), 1)
-        kept = jnp.where(lane < HEAD_DIM, rows[:, :128].astype(F32), 0.0)
-        moved = pltpu.roll(kept, HEAD_DIM, 1).astype(BF16)
-        return jnp.concatenate([moved, jnp.zeros_like(moved)], axis=1)
-
-    near = pick(side * HALF, parity)
-    near_off = pick(side * HALF, 1 - parity)
-    far = pick((1 - side) * HALF, parity)
+        target[:, :128] = left[place, :].astype(BF16)
+        target[:, 128:] = right[place, :].astype(BF16)
+
+    pick(near_ref, side * HALF, parity)
+    pick(off_ref, side * HALF, 1 - parity)
+    pick(far_ref, (1 - side) * HALF, parity)
+
+
+def as_queries(rows):
+    lane = lax.broadcasted_iota(jnp.int32, (HALF // 2, 128), 1)
+    kept = jnp.where(lane < HEAD_DIM, rows[:, :128].astype(F32), 0.0)
+    moved = pltpu.roll(kept, HEAD_DIM, 1).astype(BF16)
+    return jnp.concatenate([moved, jnp.zeros_like(moved)], axis=1)
+
+
+def attention_kernel(
+    near_ref,
+    off_ref,
+    far_ref,
+    gain_ref,
+    weight_ref,
+    out_ref,
+    tiles_ref,
+    inbox,
+    own_sem,
+    send_sem,
+    recv_sem,
+):
+    group = lax.axis_index("groups")
+    me = lax.axis_index("seq")
+    head, side = me // 2, lax.rem(me, 2)
+    parity, shift = lax.rem(head, 2), head // 2
+    home_side = me // HEADS
+    barrier = pltpu.get_barrier_semaphore()
+    for h in range(HEADS):
+
+        @pl.when(2 * h + home_side != me)
+        def _():
+            pl.semaphore_signal(
+                barrier, inc=1, device_id=(group, 2 * h + home_side), device_id_type=MESH
+            )
+
+    near, near_off, far = near_ref[...], off_ref[...], far_ref[...]
     count = HALF // 2
     key_depth = shared_depth(lax.broadcasted_iota(jnp.int32, (count, 1), 0), shift)
     query_depth = shared_depth(lax.broadcasted_iota(jnp.int32, (1, count), 1), shift)
@@ -418,25 +448,9 @@
     odd = jnp.where(parity == 0, off, same).astype(BF16)
     for t in range(HALF // TILE_DEV):
         low = t * (TILE_DEV // 2)
-        out_ref[t] = jnp.concatenate(
+        tiles_ref[t] = jnp.concatenate(
             [even[:, low : low + TILE_DEV // 2], odd[:, low : low + TILE_DEV // 2]], axis=1
         )
-
-
-def project_kernel(tiles_ref, gain_ref, weight_ref, out_ref, inbox, own_sem, send_sem, recv_sem):
-    group = lax.axis_index("groups")
-    me = lax.axis_index("seq")
-    head, side = me // 2, lax.rem(me, 2)
-    home_side = me // HEADS
-    barrier = pltpu.get_barrier_semaphore()
-    for h in range(HEADS):
-
-        @pl.when(2 * h + home_side != me)
-        def _():
-            pl.semaphore_signal(
-                barrier, inc=1, device_id=(group, 2 * h + home_side), device_id_type=MESH
-            )
-
     pl.semaphore_wait(barrier, HEADS - jnp.where(side == home_side, 1, 0))
 
     def remote(t):
@@ -527,13 +541,14 @@
     slots = tile_heads.shape[0]
     vmem = pl.BlockSpec(memory_space=pltpu.VMEM)
     smem = pl.BlockSpec(memory_space=pltpu.SMEM)
-    hbm = pl.BlockSpec(memory_space=pl.ANY)
+    hbm = pl.BlockSpec(memory_space=pltpu.HBM)
+    anywhere = pl.BlockSpec(memory_space=pl.ANY)
     dma = pltpu.SemaphoreType.DMA
     pieces = pl.pallas_call(
         encode_kernel,
         out_shape=jax.ShapeDtypeStruct((devices, HALVES, PIECE, slots // HALVES), BF16),
         in_specs=[hbm] * 2 + [vmem] * 5 + [hbm] * 3,
-        out_specs=vmem,
+        out_specs=anywhere,
         scratch_shapes=[
             pltpu.VMEM(tile_heads.shape, BF16),
             pltpu.VMEM(tile_stream.shape, BF16),
@@ -562,32 +577,34 @@
         embed_weight,
         triple_weight,
     )
-    tiles = pl.pallas_call(
-        attention_kernel,
-        out_shape=jax.ShapeDtypeStruct((HEADS, HEAD_DIM, TILE_DEV), BF16),
+    listed = jax.ShapeDtypeStruct((HALF // 2, 256), BF16)
+    near, off, far = pl.pallas_call(
+        compact_kernel,
+        out_shape=(listed, listed, listed),
         in_specs=[smem, vmem],
-        out_specs=vmem,
+        out_specs=(vmem, vmem, vmem),
         scratch_shapes=[
             pltpu.VMEM((2 * HALF + slots, 128), F32),
             pltpu.VMEM((2 * HALF + slots, 128), F32),
         ],
-        compiler_params=pltpu.CompilerParams(vmem_limit_bytes=40 * MIB),
+        compiler_params=pltpu.CompilerParams(vmem_limit_bytes=24 * MIB),
     )(tissue_counts, pieces)
     return pl.pallas_call(
-        project_kernel,
+        attention_kernel,
         out_shape=jax.ShapeDtypeStruct((TILE_DEV, output_weight.shape[1]), BF16),
-        in_specs=[vmem] * 3,
+        in_specs=[vmem] * 5,
         out_specs=vmem,
         scratch_shapes=[
+            pltpu.VMEM((HEADS, HEAD_DIM, TILE_DEV), BF16),
             pltpu.VMEM((HEADS, HEAD_DIM, TILE_DEV), BF16),
             dma,
             dma((HEADS,)),
             dma((HEADS,)),
         ],
         compiler_params=pltpu.CompilerParams(
-            collective_id=1, has_side_effects=True, vmem_limit_bytes=16 * MIB
+            collective_id=1, has_side_effects=True, vmem_limit_bytes=32 * MIB
         ),
-    )(tiles, inner_gain[:, None], output_weight)
+    )(near, off, far, inner_gain[:, None], output_weight)
 
 
 def solution(mesh):

time: 40 us -> 36.5 us (0.912)
  Pallas kernels: 37.7 us -> 34.3 us
    pallas_call x2, Pallas kernels: 11.8 us -> 9.05 us  [the longest x1 7.58 us: local(): pl.pallas_call(attention_kernel, out_shape=jax.ShapeDtypeStruct((TILE_DEV...]
    pallas_call x1, Pallas kernels: 25.9 us -> 25.3 us  [local(): pl.pallas_call(encode_kernel, out_shape=jax.ShapeDtypeStruct((devices, HA...]
where the time goes in v3:
time: 36.5 us
  Pallas kernels  34.3 us (94%)
  local copies, waits for them, and re-layouts  2.06 us (6%)
    pallas_call x1, Pallas kernels, local(): pl.pallas_call(encode_kernel, out_shape=jax.ShapeDtypeStruct((devices, HA...  25.3 us
    pallas_call x1, Pallas kernels, local(): pl.pallas_call(attention_kernel, out_shape=jax.ShapeDtypeStruct((TILE_DEV...  7.58 us
    unnamed x9, local copies, waits for them, and re-layouts  1.95 us
    pallas_call x1, Pallas kernels, local(): pl.pallas_call(compact_kernel, out_shape=(listed, listed, listed), in_spe...  1.47 us

profile of v3, /device:TPU:0, one launch (start us, length us, event | category | flops | bytes accessed | tf_op | source)
XLA Modules:
  0.0 36.5 jit_solution(1019150865894186321)
XLA Ops:
  0.0 0.0 copy-start.2
  0.0 0.0 copy-start.3
  0.0 0.0 copy-start.1
  0.0 25.3 %shard_map.127.pieces = bf16[16,2,144,128]{3,2,1,0:T(8,128)(2,1)} custom-call(bf16[256,1536]{1,0:T(8,128)(2,1)} %heads_hbm.1, bf16[256,1536]{1,0:T(8,128)(2,1)} %stream_hbm.1, f32[1536]{0:T(1024)} %scale_ref.1, f32[1536]{0:T(1024)} %gain_ref.1, f32[1536]{0:T(1024)} %bias_ref.1, f32[768]{0:T(1024)} %embed_bias_ref.1, f32[768]{0:T(1024)} %slide_gain_ref.1, ...), custom_call_target="tpu_custom_call" | custom-call | tf_op jit(solution)/shard_map/pallas_call | solution.py:547
  25.3 0.0 copy-done.2
  25.3 0.0 copy-start
  25.3 1.3 %copy-done = bf16[16,2,144,128]{3,2,1,0:T(8,128)(2,1)S(1)} copy-done((bf16[16,2,144,128]{3,2,1,0:T(8,128)(2,1)S(1)}, bf16[16,2,144,128]{3,2,1,0:T(8,128)(2,1)}, u32[]{:S(2)}) %copy-start) | copy-done | bytes 1179672
  26.6 1.5 %shard_map.128 = (bf16[512,256]{1,0:T(8,128)(2,1)S(1)}, bf16[512,256]{1,0:T(8,128)(2,1)S(1)}, bf16[512,256]{1,0:T(8,128)(2,1)S(1)}) custom-call(s32[16]{0:T(128)S(1)} %copy-done.2, bf16[16,2,144,128]{3,2,1,0:T(8,128)(2,1)S(1)} %copy-done), custom_call_target="tpu_custom_call" | custom-call | tf_op jit(solution)/shard_map/pallas_call | solution.py:581
  28.1 0.0 copy-done.3
  28.1 0.1 broadcast_in_dim.4.gain_ref
  28.2 0.0 copy-done.1
  28.2 7.6 %shard_map.129 = bf16[128,768]{1,0:T(8,128)(2,1)S(1)} custom-call(bf16[512,256]{1,0:T(8,128)(2,1)S(1)} %get-tuple-element.8.near_ref, bf16[512,256]{1,0:T(8,128)(2,1)S(1)} %get-tuple-element.9.off_ref, bf16[512,256]{1,0:T(8,128)(2,1)S(1)} %get-tuple-element.10.far_ref, f32[384,1]{1,0:T(8,128)S(1)} %broadcast_in_dim.4.gain_ref, bf16[384,768]{1,0:T(8,128)(2,1)S(1)} %copy-done.1), custom_call_target="tpu_custom_call" | custom-call | tf_op jit(solution)/shard_map/pallas_call | solution.py:592
  35.8 0.7 %copy.16 = bf16[128,768]{1,0:T(8,128)(2,1)} copy(bf16[128,768]{1,0:T(8,128)(2,1)S(1)} %shard_map.129) | data formatting | bytes 393216
Async XLA Ops:
  0.0 25.3 %copy-start.2 = (s32[16]{0:T(128)S(1)}, s32[16]{0:T(128)}, u32[]{:S(2)}) copy-start(s32[16]{0:T(128)} %counts_ref.1) | copy-start | bytes 196
  0.0 28.1 %copy-start.3 = (f32[384]{0:T(512)S(1)}, f32[384]{0:T(512)}, u32[]{:S(2)}) copy-start(f32[384]{0:T(512)} %param.24) | copy-start | bytes 4612
  0.0 28.2 %copy-start.1 = (bf16[384,768]{1,0:T(8,128)(2,1)S(1)}, bf16[384,768]{1,0:T(8,128)(2,1)}, u32[]{:S(2)}) copy-start(bf16[384,768]{1,0:T(8,128)(2,1)} %weight_ref.1) | copy-start | bytes 1769476
  25.3 1.3 %copy-start = (bf16[16,2,144,128]{3,2,1,0:T(8,128)(2,1)S(1)}, bf16[16,2,144,128]{3,2,1,0:T(8,128)(2,1)}, u32[]{:S(2)}) copy-start(bf16[16,2,144,128]{3,2,1,0:T(8,128)(2,1)} %shard_map.127.pieces) | copy-start | bytes 3538948

commit v4 on v3

--- a/solution.py
+++ b/solution.py
@@ -203,27 +203,34 @@
 
 ROUTE = (4, 3, 5, 2, 6, 1, 7)
 HALVES = 2
+PARTS = 2
 
 
 def encode_kernel(
     heads_hbm,
     stream_hbm,
-    scale_ref,
-    gain_ref,
-    bias_ref,
-    embed_bias_ref,
-    slide_gain_ref,
+    scale_hbm,
+    gain_hbm,
+    bias_hbm,
+    embed_bias_hbm,
+    slide_gain_hbm,
     head_weight_hbm,
     embed_weight_hbm,
     triple_weight_hbm,
     recv_ref,
     heads,
     stream,
+    scale_ref,
+    gain_ref,
+    bias_ref,
+    embed_bias_ref,
+    slide_gain_ref,
     head_weight,
     embed_weight,
     triple_weight,
     outbox,
     load_sem,
+    vector_sem,
     own_sem,
     send_sem,
     pass_sem,
@@ -238,35 +245,39 @@
     part = depth // 4
     rows = heads.shape[0] // HALVES
 
-    def load(source, target, first, count, sem):
-        copy = pltpu.make_async_copy(
-            source.at[pl.ds(first, count)], target.at[pl.ds(first, count)], load_sem.at[sem]
-        )
-        copy.start()
-        return copy
-
-    head_loads = [load(heads_hbm, heads, 0, rows, 0)]
-    weight_loads = [
-        load(head_weight_hbm, head_weight, i * part, part, 1 + i) for i in range(4)
-    ]
-    stream_loads = [load(stream_hbm, stream, 0, rows, 5)]
-    embed_load = load(embed_weight_hbm, embed_weight, 0, embed_weight.shape[0], 6)
-    triple_load = load(triple_weight_hbm, triple_weight, 0, triple_weight.shape[0], 7)
-    head_loads.append(load(heads_hbm, heads, rows, rows, 8))
-    stream_loads.append(load(stream_hbm, stream, rows, rows, 9))
-
     barrier = pltpu.get_barrier_semaphore()
     for off in range(1, chips):
         peer = 2 * lax.rem(chip + off, chips) + core
         pl.semaphore_signal(barrier, inc=1, device_id=(group, peer), device_id_type=MESH)
     pl.semaphore_signal(barrier, inc=1, device_id=(group, sibling), device_id_type=MESH)
 
+    def load(source, target, first, count, sem):
+        copy = pltpu.make_async_copy(
+            source.at[pl.ds(first, count)], target.at[pl.ds(first, count)], load_sem.at[sem]
+        )
+        copy.start()
+        return copy
+
+    head_loads = [load(heads_hbm, heads, 0, rows, 0)]
+    weight_loads = [
+        load(head_weight_hbm, head_weight, i * part, part, 1 + i) for i in range(4)
+    ]
+    stream_loads = []
+    vector_loads = []
+    for place, (source, target) in enumerate(
+        (
+            (scale_hbm, scale_ref),
+            (gain_hbm, gain_ref),
+            (bias_hbm, bias_ref),
+            (embed_bias_hbm, embed_bias_ref),
+            (slide_gain_hbm, slide_gain_ref),
+        )
+    ):
+        copy = pltpu.make_async_copy(source, target, vector_sem.at[place])
+        copy.start()
+        vector_loads.append(copy)
+
     inner = HEADS * HEAD_DIM
-    scale = scale_ref[...].reshape(1, -1)
-    gain = gain_ref[...].reshape(1, -1)
-    bias = bias_ref[...].reshape(1, -1)
-    embed_bias = embed_bias_ref[...].reshape(1, -1)
-    slide_gain = slide_gain_ref[...].reshape(1, -1)
     sends = []
     owns = []
     for half in range(HALVES):
@@ -276,12 +287,27 @@
         for i in range(4):
             if half == 0:
                 weight_loads[i].wait()
+                if i == 0:
+                    stream_loads.append(load(stream_hbm, stream, 0, rows, 5))
+                    embed_load = load(embed_weight_hbm, embed_weight, 0, embed_weight.shape[0], 6)
+                if i == 2:
+                    triple_load = load(
+                        triple_weight_hbm, triple_weight, 0, triple_weight.shape[0], 7
+                    )
             term = jnp.dot(
                 heads[low : low + rows, i * part : (i + 1) * part],
                 head_weight[i * part : (i + 1) * part, :],
                 preferred_element_type=F32,
             )
             blended = term if blended is None else blended + term
+        if half == 0:
+            for copy in vector_loads:
+                copy.wait()
+            scale = scale_ref[...].reshape(1, -1)
+            gain = gain_ref[...].reshape(1, -1)
+            bias = bias_ref[...].reshape(1, -1)
+            embed_bias = embed_bias_ref[...].reshape(1, -1)
+            slide_gain = slide_gain_ref[...].reshape(1, -1)
         stream_loads[half].wait()
         summed = stream[low : low + rows, :].astype(F32) + scale * blended
         embedding = (layer_norm(summed, gain) + bias).astype(BF16)
@@ -293,6 +319,8 @@
         normed = layer_norm(slide_rows.astype(F32), slide_gain).astype(BF16)
         if half == 0:
             triple_load.wait()
+            head_loads.append(load(heads_hbm, heads, rows, rows, 8))
+            stream_loads.append(load(stream_hbm, stream, rows, rows, 9))
         triple = jnp.dot(normed, triple_weight[...], preferred_element_type=F32)
         turned = triple.T.astype(BF16)
         for h in range(HEADS):
@@ -356,7 +384,7 @@
 
 
 def attend(keys, queries, multiplicity):
-    scaling = 1.0 / math.sqrt(HEAD_DIM)
+    scaling = math.log2(math.e) / math.sqrt(HEAD_DIM)
     scores = [
         lax.dot_general(block, queries, NT, preferred_element_type=F32) for block in keys
     ]
@@ -365,7 +393,7 @@
         highest = jnp.maximum(highest, block.max(axis=0, keepdims=True))
     total = blended = None
     for block, values, times in zip(scores, keys, multiplicity):
-        weights = jnp.exp((block - highest) * scaling)
+        weights = jnp.exp2((block - highest) * scaling)
         if times is not None:
             weights = weights * times
         part_total = weights.sum(axis=0, keepdims=True)
@@ -437,22 +465,6 @@
                 barrier, inc=1, device_id=(group, 2 * h + home_side), device_id_type=MESH
             )
 
-    near, near_off, far = near_ref[...], off_ref[...], far_ref[...]
-    count = HALF // 2
-    key_depth = shared_depth(lax.broadcasted_iota(jnp.int32, (count, 1), 0), shift)
-    query_depth = shared_depth(lax.broadcasted_iota(jnp.int32, (1, count), 1), shift)
-    times = jnp.minimum(key_depth, query_depth).astype(F32)
-    same = attend([near, near_off, far], as_queries(near), [times + 1.0, None, times])
-    off = attend([near, near_off], as_queries(near_off), [None, None])
-    even = jnp.where(parity == 0, same, off).astype(BF16)
-    odd = jnp.where(parity == 0, off, same).astype(BF16)
-    for t in range(HALF // TILE_DEV):
-        low = t * (TILE_DEV // 2)
-        tiles_ref[t] = jnp.concatenate(
-            [even[:, low : low + TILE_DEV // 2], odd[:, low : low + TILE_DEV // 2]], axis=1
-        )
-    pl.semaphore_wait(barrier, HEADS - jnp.where(side == home_side, 1, 0))
-
     def remote(t):
         return pltpu.make_async_remote_copy(
             src_ref=tiles_ref.at[t],
@@ -463,17 +475,46 @@
             device_id_type=MESH,
         )
 
-    for t in range(HEADS):
-
-        @pl.when(side * HEADS + t != me)
-        def _():
-            remote(t).start()
-
-        @pl.when(side * HEADS + t == me)
-        def _():
-            own = pltpu.make_async_copy(tiles_ref.at[t], inbox.at[head], own_sem)
-            own.start()
-            own.wait()
+    near, near_off, far = near_ref[...], off_ref[...], far_ref[...]
+    count = HALF // 2
+    key_depth = shared_depth(lax.broadcasted_iota(jnp.int32, (count, 1), 0), shift)
+    query_depth = shared_depth(lax.broadcasted_iota(jnp.int32, (1, count), 1), shift)
+    times = jnp.minimum(key_depth, query_depth).astype(F32)
+    near_queries, off_queries = as_queries(near), as_queries(near_off)
+    per = TILE_DEV // 2
+    span = count // PARTS
+    for part in range(PARTS):
+        low = part * span
+        part_times = times[:, low : low + span]
+        same = attend(
+            [near, near_off, far],
+            near_queries[low : low + span, :],
+            [part_times + 1.0, None, part_times],
+        )
+        off = attend([near, near_off], off_queries[low : low + span, :], [None, None])
+        even = jnp.where(parity == 0, same, off).astype(BF16)
+        odd = jnp.where(parity == 0, off, same).astype(BF16)
+        if part == 0:
+            pl.semaphore_wait(barrier, HEADS - jnp.where(side == home_side, 1, 0))
+        for place in range(span // per):
+            t = part * (span // per) + place
+            tiles_ref[t] = jnp.concatenate(
+                [
+                    even[:, place * per : (place + 1) * per],
+                    odd[:, place * per : (place + 1) * per],
+                ],
+                axis=1,
+            )
+
+            @pl.when(side * HEADS + t != me)
+            def _():
+                remote(t).start()
+
+            @pl.when(side * HEADS + t == me)
+            def _():
+                own = pltpu.make_async_copy(tiles_ref.at[t], inbox.at[head], own_sem)
+                own.start()
+                own.wait()
 
     for h in range(HEADS):
 
@@ -541,22 +582,27 @@
     slots = tile_heads.shape[0]
     vmem = pl.BlockSpec(memory_space=pltpu.VMEM)
     smem = pl.BlockSpec(memory_space=pltpu.SMEM)
-    hbm = pl.BlockSpec(memory_space=pltpu.HBM)
     anywhere = pl.BlockSpec(memory_space=pl.ANY)
     dma = pltpu.SemaphoreType.DMA
     pieces = pl.pallas_call(
         encode_kernel,
         out_shape=jax.ShapeDtypeStruct((devices, HALVES, PIECE, slots // HALVES), BF16),
-        in_specs=[hbm] * 2 + [vmem] * 5 + [hbm] * 3,
+        in_specs=[anywhere] * 10,
         out_specs=anywhere,
         scratch_shapes=[
             pltpu.VMEM(tile_heads.shape, BF16),
             pltpu.VMEM(tile_stream.shape, BF16),
+            pltpu.VMEM(stream_scale.shape, F32),
+            pltpu.VMEM(final_gain.shape, F32),
+            pltpu.VMEM(final_bias.shape, F32),
+            pltpu.VMEM(embed_bias.shape, F32),
+            pltpu.VMEM(slide_gain.shape, F32),
             pltpu.VMEM(head_weight.shape, BF16),
             pltpu.VMEM(embed_weight.shape, BF16),
             pltpu.VMEM(triple_weight.shape, BF16),
             pltpu.VMEM((HALVES, HEADS, PIECE, slots // HALVES), BF16),
             dma((10,)),
+            dma((5,)),
             dma((HALVES,)),
             dma((HALVES, HEADS)),
             dma((HALVES, HEADS)),

time: 36.5 us -> 36.1 us (0.989)
  Pallas kernels: 34.3 us -> 33.8 us
where the time goes in v4:
time: 36.1 us; the launch traced here: 35.9 us
  Pallas kernels  33.8 us (94%)
  local copies, waits for them, and re-layouts  2.06 us (6%)
    pallas_call x1, Pallas kernels, local(): pl.pallas_call(encode_kernel, out_shape=jax.ShapeDtypeStruct((devices, HA...  25 us
    pallas_call x1, Pallas kernels, local(): pl.pallas_call(attention_kernel, out_shape=jax.ShapeDtypeStruct((TILE_DEV...  7.38 us
    unnamed x9, local copies, waits for them, and re-layouts  1.95 us
    pallas_call x1, Pallas kernels, local(): pl.pallas_call(compact_kernel, out_shape=(listed, listed, listed), in_spe...  1.47 us

profile of v4, /device:TPU:0, one launch (start us, length us, event | category | flops | bytes accessed | tf_op | source)
XLA Modules:
  0.0 35.9 jit_solution(1609216557887859090)
XLA Ops:
  0.0 0.0 copy-start.2
  0.0 0.0 copy-start.3
  0.0 0.0 copy-start.1
  0.0 25.0 %shard_map.127.pieces = bf16[16,2,144,128]{3,2,1,0:T(8,128)(2,1)} custom-call(bf16[256,1536]{1,0:T(8,128)(2,1)} %heads_hbm.1, bf16[256,1536]{1,0:T(8,128)(2,1)} %stream_hbm.1, f32[1536]{0:T(1024)} %scale_hbm.1, f32[1536]{0:T(1024)} %gain_hbm.1, f32[1536]{0:T(1024)} %bias_hbm.1, f32[768]{0:T(1024)} %embed_bias_hbm.1, f32[768]{0:T(1024)} %slide_gain_hbm.1, ...), custom_call_target="tpu_custom_call" | custom-call | tf_op jit(solution)/shard_map/pallas_call | solution.py:587
  25.0 0.0 copy-done.2
  25.0 0.0 copy-start
  25.0 1.3 %copy-done = bf16[16,2,144,128]{3,2,1,0:T(8,128)(2,1)S(1)} copy-done((bf16[16,2,144,128]{3,2,1,0:T(8,128)(2,1)S(1)}, bf16[16,2,144,128]{3,2,1,0:T(8,128)(2,1)}, u32[]{:S(2)}) %copy-start) | copy-done | bytes 1179672
  26.3 1.5 %shard_map.128 = (bf16[512,256]{1,0:T(8,128)(2,1)S(1)}, bf16[512,256]{1,0:T(8,128)(2,1)S(1)}, bf16[512,256]{1,0:T(8,128)(2,1)S(1)}) custom-call(s32[16]{0:T(128)S(1)} %copy-done.2, bf16[16,2,144,128]{3,2,1,0:T(8,128)(2,1)S(1)} %copy-done), custom_call_target="tpu_custom_call" | custom-call | tf_op jit(solution)/shard_map/pallas_call | solution.py:627
  27.7 0.0 copy-done.3
  27.7 0.1 broadcast_in_dim.4.gain_ref
  27.9 0.0 copy-done.1
  27.9 7.4 %shard_map.129 = bf16[128,768]{1,0:T(8,128)(2,1)S(1)} custom-call(bf16[512,256]{1,0:T(8,128)(2,1)S(1)} %get-tuple-element.8.near_ref, bf16[512,256]{1,0:T(8,128)(2,1)S(1)} %get-tuple-element.9.off_ref, bf16[512,256]{1,0:T(8,128)(2,1)S(1)} %get-tuple-element.10.far_ref, f32[384,1]{1,0:T(8,128)S(1)} %broadcast_in_dim.4.gain_ref, bf16[384,768]{1,0:T(8,128)(2,1)S(1)} %copy-done.1), custom_call_target="tpu_custom_call" | custom-call | tf_op jit(solution)/shard_map/pallas_call | solution.py:638
  35.3 0.7 %copy.16 = bf16[128,768]{1,0:T(8,128)(2,1)} copy(bf16[128,768]{1,0:T(8,128)(2,1)S(1)} %shard_map.129) | data formatting | bytes 393216
Async XLA Ops:
  0.0 25.0 %copy-start.2 = (s32[16]{0:T(128)S(1)}, s32[16]{0:T(128)}, u32[]{:S(2)}) copy-start(s32[16]{0:T(128)} %counts_ref.1) | copy-start | bytes 196
  0.0 27.7 %copy-start.3 = (f32[384]{0:T(512)S(1)}, f32[384]{0:T(512)}, u32[]{:S(2)}) copy-start(f32[384]{0:T(512)} %param.24) | copy-start | bytes 4612
  0.0 27.9 %copy-start.1 = (bf16[384,768]{1,0:T(8,128)(2,1)S(1)}, bf16[384,768]{1,0:T(8,128)(2,1)}, u32[]{:S(2)}) copy-start(bf16[384,768]{1,0:T(8,128)(2,1)} %weight_ref.1) | copy-start | bytes 1769476
  25.0 1.3 %copy-start = (bf16[16,2,144,128]{3,2,1,0:T(8,128)(2,1)S(1)}, bf16[16,2,144,128]{3,2,1,0:T(8,128)(2,1)}, u32[]{:S(2)}) copy-start(bf16[16,2,144,128]{3,2,1,0:T(8,128)(2,1)} %shard_map.127.pieces) | copy-start | bytes 3538948

commit v5 on v4

--- a/solution.py
+++ b/solution.py
@@ -383,7 +383,7 @@
     return jnp.where(residue & 1 != 0, 1, depth)
 
 
-def attend(keys, queries, multiplicity):
+def attend(keys, turned, queries, multiplicity):
     scaling = math.log2(math.e) / math.sqrt(HEAD_DIM)
     scores = [
         lax.dot_general(block, queries, NT, preferred_element_type=F32) for block in keys
@@ -392,15 +392,15 @@
     for block in scores[1:]:
         highest = jnp.maximum(highest, block.max(axis=0, keepdims=True))
     total = blended = None
-    for block, values, times in zip(scores, keys, multiplicity):
+    for block, values, times in zip(scores, turned, multiplicity):
         weights = jnp.exp2((block - highest) * scaling)
         if times is not None:
             weights = weights * times
         part_total = weights.sum(axis=0, keepdims=True)
-        part = lax.dot_general(values, weights.astype(BF16), TN, preferred_element_type=F32)
+        part = jnp.dot(values, weights.astype(BF16), preferred_element_type=F32)
         total = part_total if total is None else total + part_total
         blended = part if blended is None else blended + part
-    return blended[2 * HEAD_DIM : PIECE, :] / total
+    return blended / total
 
 
 def compact_kernel(counts_ref, pieces, near_ref, off_ref, far_ref, left, right):
@@ -481,6 +481,7 @@
     query_depth = shared_depth(lax.broadcasted_iota(jnp.int32, (1, count), 1), shift)
     times = jnp.minimum(key_depth, query_depth).astype(F32)
     near_queries, off_queries = as_queries(near), as_queries(near_off)
+    near_t, off_t, far_t = [rows.T[2 * HEAD_DIM : PIECE, :] for rows in (near, near_off, far)]
     per = TILE_DEV // 2
     span = count // PARTS
     for part in range(PARTS):
@@ -488,10 +489,13 @@
         part_times = times[:, low : low + span]
         same = attend(
             [near, near_off, far],
+            [near_t, off_t, far_t],
             near_queries[low : low + span, :],
             [part_times + 1.0, None, part_times],
         )
-        off = attend([near, near_off], off_queries[low : low + span, :], [None, None])
+        off = attend(
+            [near, near_off], [near_t, off_t], off_queries[low : low + span, :], [None, None]
+        )
         even = jnp.where(parity == 0, same, off).astype(BF16)
         odd = jnp.where(parity == 0, off, same).astype(BF16)
         if part == 0:

time: 36.1 us -> 36 us (level)
  no operation moved by 1% of the time
where the time goes in v5:
time: 36 us; the launch traced here: 35.9 us
  Pallas kernels  33.8 us (94%)
  local copies, waits for them, and re-layouts  2.06 us (6%)
    pallas_call x1, Pallas kernels, local(): pl.pallas_call(encode_kernel, out_shape=jax.ShapeDtypeStruct((devices, HA...  25 us
    pallas_call x1, Pallas kernels, local(): pl.pallas_call(attention_kernel, out_shape=jax.ShapeDtypeStruct((TILE_DEV...  7.33 us
    unnamed x9, local copies, waits for them, and re-layouts  1.95 us
    pallas_call x1, Pallas kernels, local(): pl.pallas_call(compact_kernel, out_shape=(listed, listed, listed), in_spe...  1.47 us

profile of v5, /device:TPU:0, one launch (start us, length us, event | category | flops | bytes accessed | tf_op | source)
XLA Modules:
  0.0 35.9 jit_solution(17781499478173331659)
XLA Ops:
  0.0 0.0 copy-start.2
  0.0 0.0 copy-start.3
  0.0 0.0 copy-start.1
  0.0 25.0 %shard_map.127.pieces = bf16[16,2,144,128]{3,2,1,0:T(8,128)(2,1)} custom-call(bf16[256,1536]{1,0:T(8,128)(2,1)} %heads_hbm.1, bf16[256,1536]{1,0:T(8,128)(2,1)} %stream_hbm.1, f32[1536]{0:T(1024)} %scale_hbm.1, f32[1536]{0:T(1024)} %gain_hbm.1, f32[1536]{0:T(1024)} %bias_hbm.1, f32[768]{0:T(1024)} %embed_bias_hbm.1, f32[768]{0:T(1024)} %slide_gain_hbm.1, ...), custom_call_target="tpu_custom_call" | custom-call | tf_op jit(solution)/shard_map/pallas_call | solution.py:591
  25.0 0.0 copy-done.2
  25.0 0.0 copy-start
  25.0 1.3 %copy-done = bf16[16,2,144,128]{3,2,1,0:T(8,128)(2,1)S(1)} copy-done((bf16[16,2,144,128]{3,2,1,0:T(8,128)(2,1)S(1)}, bf16[16,2,144,128]{3,2,1,0:T(8,128)(2,1)}, u32[]{:S(2)}) %copy-start) | copy-done | bytes 1179672
  26.3 1.5 %shard_map.128 = (bf16[512,256]{1,0:T(8,128)(2,1)S(1)}, bf16[512,256]{1,0:T(8,128)(2,1)S(1)}, bf16[512,256]{1,0:T(8,128)(2,1)S(1)}) custom-call(s32[16]{0:T(128)S(1)} %copy-done.2, bf16[16,2,144,128]{3,2,1,0:T(8,128)(2,1)S(1)} %copy-done), custom_call_target="tpu_custom_call" | custom-call | tf_op jit(solution)/shard_map/pallas_call | solution.py:631
  27.7 0.0 copy-done.3
  27.7 0.1 broadcast_in_dim.4.gain_ref
  27.9 0.0 copy-done.1
  27.9 7.3 %shard_map.129 = bf16[128,768]{1,0:T(8,128)(2,1)S(1)} custom-call(bf16[512,256]{1,0:T(8,128)(2,1)S(1)} %get-tuple-element.8.near_ref, bf16[512,256]{1,0:T(8,128)(2,1)S(1)} %get-tuple-element.9.off_ref, bf16[512,256]{1,0:T(8,128)(2,1)S(1)} %get-tuple-element.10.far_ref, f32[384,1]{1,0:T(8,128)S(1)} %broadcast_in_dim.4.gain_ref, bf16[384,768]{1,0:T(8,128)(2,1)S(1)} %copy-done.1), custom_call_target="tpu_custom_call" | custom-call | tf_op jit(solution)/shard_map/pallas_call | solution.py:642
  35.2 0.7 %copy.16 = bf16[128,768]{1,0:T(8,128)(2,1)} copy(bf16[128,768]{1,0:T(8,128)(2,1)S(1)} %shard_map.129) | data formatting | bytes 393216
Async XLA Ops:
  0.0 25.0 %copy-start.2 = (s32[16]{0:T(128)S(1)}, s32[16]{0:T(128)}, u32[]{:S(2)}) copy-start(s32[16]{0:T(128)} %counts_ref.1) | copy-start | bytes 196
  0.0 27.7 %copy-start.3 = (f32[384]{0:T(512)S(1)}, f32[384]{0:T(512)}, u32[]{:S(2)}) copy-start(f32[384]{0:T(512)} %param.24) | copy-start | bytes 4612
  0.0 27.9 %copy-start.1 = (bf16[384,768]{1,0:T(8,128)(2,1)S(1)}, bf16[384,768]{1,0:T(8,128)(2,1)}, u32[]{:S(2)}) copy-start(bf16[384,768]{1,0:T(8,128)(2,1)} %weight_ref.1) | copy-start | bytes 1769476
  25.0 1.3 %copy-start = (bf16[16,2,144,128]{3,2,1,0:T(8,128)(2,1)S(1)}, bf16[16,2,144,128]{3,2,1,0:T(8,128)(2,1)}, u32[]{:S(2)}) copy-start(bf16[16,2,144,128]{3,2,1,0:T(8,128)(2,1)} %shard_map.127.pieces) | copy-start | bytes 3538948
